TPU v7x, 512 devices: a whole 4x4x16 slice. The times are simulated.
512 devices in a mesh: item: 32 (over y, z_hi, core), code: 16 (over z_lo, x).
Axes of the slice: x: 4, y: 4, z: 16 (z_hi: 4, z_lo: 4; z = z_hi * 4 + z_lo), core: 2. Of those that a mesh axis runs over, the one named last changes fastest.
Arguments:
- embeddings: bfloat16 [512, 262144], P('code', 'item'), may hold values from -6 to 6
- first_codes: int32 [262144], P('item'), may hold values from 0 to 8191
- second_codes: int32 [262144], P('item'), may hold values from 0 to 8191
- first_old: float32 [512, 8192], P('code', 'item'), may hold values from -6 to 6
- second_old: float32 [512, 8192], P('code', 'item'), may hold values from -3 to 3
Outputs:
- first_new: float32 [512, 8192], P('code', 'item')
- second_new: float32 [512, 8192], P('code', 'item')
- leftover: float32 [512, 262144], P('code', 'item')
All inputs are finite; a program needn't handle non-finite values.
Results may differ from a plain program's by a relative error of at most 0.0003.
Values sent between devices are 32-bit elements; how exact they have to be, the bound alone decides.
No kernel may reach another device: no remote copies, remote signals or barrier semaphores. Data moves between devices by JAX's collectives and lax.ppermute only.
A program may use at most 64 MiB of HBM per device.

v0:
```python
import jax
import jax.numpy as jnp
from jax import lax
from jax.sharding import PartitionSpec as P

D = 512
K = 8192


def level_update(columns, codes, old):
    sums = jax.ops.segment_sum(columns.T, codes, num_segments=K).T
    counts = jax.ops.segment_sum(jnp.ones(codes.shape, jnp.float32), codes, num_segments=K)[None, :]
    own_sums, own_counts = (
        lax.psum_scatter(sums, "item", scatter_dimension=1, tiled=True),
        lax.psum_scatter(counts, "item", scatter_dimension=1, tiled=True),
    )
    own_new = 0.5 * old + 0.5 * own_sums / (own_counts + 1.0)
    whole_new = lax.all_gather(own_new, "item", axis=1, tiled=True)
    return (own_new, whole_new)


def on_device(embeddings, first_codes, second_codes, first_old, second_old):
    values = embeddings.astype(jnp.float32)
    squares = lax.psum(jnp.sum(values * values, axis=0), "code")
    normed = values * lax.rsqrt(squares / D + 1e-06)[None, :]
    first_new, first_whole = level_update(normed, first_codes, first_old)
    middle = normed - jnp.take(first_whole, first_codes, axis=1)
    second_new, second_whole = level_update(middle, second_codes, second_old)
    leftover = middle - jnp.take(second_whole, second_codes, axis=1)
    return (first_new, second_new, leftover)


def solution(mesh):
    in_specs = (P("code", "item"), P("item"), P("item"), P("code", "item"), P("code", "item"))
    out_specs = (P("code", "item"), P("code", "item"), P("code", "item"))
    return jax.shard_map(
        on_device, mesh=mesh, in_specs=in_specs, out_specs=out_specs, check_vma=False
    )
```

profile of v0, /device:TPU:1, one launch (start us, length us, event | category | flops | bytes accessed | tf_op | source)
XLA Modules:
  0.0 849.8 jit_solution(17355611729849861227)
XLA Ops:
  7.2 43.4 %scatter_custom_fusion.1 = f32[8192]{0:T(1024)S(1)} fusion(s32[8192]{0:T(1024)} %param.8, f32[8192]{0:T(1024)S(1)} %broadcast.25, f32[]{:T(128)} %constant.1.clone.1), kind=kCustom, calls=%fused_computation.34 | custom fusion | flops 8192 | bytes 33280 | tf_op jit(solution)/shard_map/scatter-add | solution.py:12
  50.6 2.7 copy.20
  53.4 1.0 copy.15
  54.4 1.2 fusion.4
  55.6 67.7 %psum.7 = f32[8192]{0:T(1024)S(1)} all-reduce(f32[8192]{0:T(1024)S(1)} %fusion.4), channel_id=1, replica_groups=mesh['item'=32,'code'=16] {'code'}, use_global_device_ids=true, to_apply=%region_1.0 | all-reduce | flops 8192 | bytes 65536 | tf_op jit(solution)/shard_map/psum | solution.py:24
  123.3 50.2 %scatter_custom_fusion = f32[8192,32]{1,0:T(8,128)} fusion(s32[8192]{0:T(1024)S(1)} %copy-done.2, bf16[32,8192]{0,1:T(8,128)(2,1)S(1)} %copy.15, f32[8192]{0:T(1024)S(1)} %add_rsqrt_fusion, f32[]{:T(128)} %constant.1.clone.1), kind=kCustom, calls=%fused_computation.10 | custom fusion | flops 786432 | bytes 3178500 | tf_op jit(solution)/shard_map/scatter-add | solution.py:11
  173.7 23.3 %reduce-scatter.13.cloned.1.call-done = f32[256,1]{1,0:T(8,128)} async-done(((f32[8192,1]{1,0:T(8,128)}), f32[256,1]{1,0:T(8,128)}) %reduce-scatter.13.cloned.1.call-update) | async-done | bytes 1040
  197.1 0.9 add_bitcast_fusion.1
  198.1 137.6 %reduce-scatter.9.cloned.1.call-done = f32[32,256]{0,1:T(8,128)} async-done(((f32[32,8192]{0,1:T(8,128)}), f32[32,256]{0,1:T(8,128)}) %reduce-scatter.9.cloned.1.call-update) | async-done | bytes 32784 | tf_op jit(solution)/shard_map/reduce_scatter | solution.py:14
  335.7 1.7 divide_add_fusion.1
  337.4 43.2 %scatter_custom_fusion.3 = f32[8192]{0:T(1024)S(1)} fusion(s32[8192]{0:T(1024)S(1)} %copy-done.3, f32[8192]{0:T(1024)S(1)} %broadcast.25, f32[]{:T(128)} %constant.1.clone.1), kind=kCustom, calls=%fused_computation.32 | custom fusion | flops 8192 | bytes 32772 | tf_op jit(solution)/shard_map/scatter-add | solution.py:12
  380.7 2.7 copy.22
  383.4 47.5 %all-gather.3.cloned.1.call-done = f32[32,8192]{0,1:T(8,128)} async-done(((f32[32,256]{0,1:T(8,128)}), f32[32,8192]{0,1:T(8,128)}) %all-gather.3.cloned.1.call-update) | async-done | bytes 1048592 | tf_op jit(solution)/shard_map/all_gather | solution.py:18
  430.9 29.9 %gather_fusion = f32[8192,32]{1,0:T(8,128)} fusion(f32[32,8192]{0,1:T(8,128)} %all-gather.3.cloned.1.call-done, s32[8192]{0:T(1024)S(1)} %fusion.14), kind=kCustom, calls=%fused_computation.clone | custom fusion | bytes 2129920 | tf_op jit(solution)/shard_map/jit(_take)/gather | solution.py:27
  460.8 47.8 %scatter_custom_fusion.2 = f32[8192,32]{1,0:T(8,128)} fusion(s32[8192]{0:T(1024)S(1)} %copy-done.3, bf16[32,8192]{0,1:T(8,128)(2,1)S(1)} %copy.15, f32[8192,32]{1,0:T(8,128)} %gather_fusion, f32[]{:T(128)} %constant.12.clone.2, f32[8192]{0:T(1024)S(1)} %add_rsqrt_fusion, f32[]{:T(128)} %constant.1.clone.1, pred[8192]{0:T(1024)(128)(4,1)S(1)} %compare_and_fusion.1), kind=kCustom, calls=%fused_computation.13 | custom fusion | flops 1310720 | bytes 4235272 | tf_op jit(solution)/shard_map/scatter-add | solution.py:11
  509.5 58.4 %reduce-scatter.15.cloned.1.call-done = f32[256,1]{1,0:T(8,128)} async-done(((f32[8192,1]{1,0:T(8,128)}), f32[256,1]{1,0:T(8,128)}) %reduce-scatter.15.cloned.1.call-update) | async-done | bytes 1040
  567.8 0.9 add_bitcast_fusion
  568.8 137.3 %reduce-scatter.11.cloned.1.call-done = f32[32,256]{0,1:T(8,128)} async-done(((f32[32,8192]{0,1:T(8,128)}), f32[32,256]{0,1:T(8,128)}) %reduce-scatter.11.cloned.1.call-update) | async-done | bytes 32784 | tf_op jit(solution)/shard_map/reduce_scatter | solution.py:14
  706.1 1.7 divide_add_fusion
  708.6 1.6 copy.18
  710.1 90.5 %all-gather.5.cloned.1.call-done = f32[32,8192]{0,1:T(8,128)} async-done(((f32[32,256]{0,1:T(8,128)}), f32[32,8192]{0,1:T(8,128)}) %all-gather.5.cloned.1.call-update) | async-done | bytes 1048592 | tf_op jit(solution)/shard_map/all_gather | solution.py:18
  800.6 29.9 %gather_fusion.1 = f32[8192,32]{1,0:T(8,128)} fusion(f32[32,8192]{0,1:T(8,128)} %all-gather.5.cloned.1.call-done, s32[8192]{0:T(1024)S(1)} %fusion.15), kind=kCustom, calls=%fused_computation.1.clone | custom fusion | bytes 2129920 | tf_op jit(solution)/shard_map/jit(_take)/gather | solution.py:29
  830.5 8.8 %bitcast_subtract_fusion = f32[32,8192]{0,1:T(8,128)} fusion(f32[8192,32]{1,0:T(8,128)} %gather_fusion.1, f32[8192,32]{1,0:T(8,128)} %gather_fusion, bf16[32,8192]{0,1:T(8,128)(2,1)S(1)} %copy.15, f32[8192]{0:T(1024)S(1)} %add_rsqrt_fusion, pred[8192]{0:T(1024)(128)(4,1)S(1)} %compare_and_fusion, pred[8192]{0:T(1024)(128)(4,1)S(1)} %compare_and_fusion.1), kind=kLoop, calls=%fused_computation.12 | loop fusion | flops 1572864 | bytes 3719168 | tf_op jit(solution)/shard_map/sub | solution.py:29
  839.4 3.6 copy.19
  (35 shorter events, 2.2 us)
Async XLA Ops:
  7.2 189.9 %reduce-scatter.13.cloned.1.call-start = ((), (), s32[]{:S(2)}) async-start(), calls=%async_computation.8 | async-start | bytes 4325376
  50.6 2.8 copy-start.1
  53.3 70.0 %copy-start.2 = (s32[8192]{0:T(1024)S(1)}, s32[8192]{0:T(1024)}, u32[]{:S(2)}) copy-start(s32[8192]{0:T(1024)} %param.8) | copy-start | bytes 98308
  53.3 282.3 %reduce-scatter.9.cloned.1.call-start = ((), (), s32[]{:S(2)}) async-start(), calls=%async_computation.4 | async-start | bytes 4325376 | tf_op jit(solution)/shard_map/reduce_scatter | solution.py:14
  123.3 50.3 %copy-start.4 = (f32[32,256]{1,0:T(8,128)S(1)}, f32[32,256]{1,0:T(8,128)}, u32[]{:S(2)}) copy-start(f32[32,256]{1,0:T(8,128)} %param.10) | copy-start | bytes 98308
  173.6 163.9 %copy-start.3 = (s32[8192]{0:T(1024)S(1)}, s32[8192]{0:T(1024)}, u32[]{:S(2)}) copy-start(s32[8192]{0:T(1024)} %param.9) | copy-start | bytes 98308
  173.6 257.4 %all-gather.3.cloned.1.call-start = ((), (), s32[]{:S(2)}) async-start(), calls=%async_computation.5 | async-start | bytes 4325376 | tf_op jit(solution)/shard_map/all_gather | solution.py:18
  337.4 230.5 %reduce-scatter.15.cloned.1.call-start = ((), (), s32[]{:S(2)}) async-start(), calls=%async_computation.9 | async-start | bytes 4325376
  383.4 322.8 %reduce-scatter.11.cloned.1.call-start = ((), (), s32[]{:S(2)}) async-start(), calls=%async_computation.6 | async-start | bytes 4325376 | tf_op jit(solution)/shard_map/reduce_scatter | solution.py:14
  508.6 0.8 copy-start.5
  508.6 199.2 %copy-start = (f32[32,256]{0,1:T(8,128)S(1)}, f32[32,256]{0,1:T(8,128)}, u32[]{:S(2)}) copy-start(f32[32,256]{0,1:T(8,128)} %divide_add_fusion.1) | copy-start | bytes 98308
  508.6 292.0 %all-gather.5.cloned.1.call-start = ((), (), s32[]{:S(2)}) async-start(), calls=%async_computation.7 | async-start | bytes 4325376 | tf_op jit(solution)/shard_map/all_gather | solution.py:18
Sparse Core Ops, SparseCore 0:
  53.4 143.5 reduce-scatter.12
  202.3 133.3 reduce-scatter.8
  339.4 91.5 all-gather.2
  435.3 132.4 reduce-scatter.14
  572.8 133.2 reduce-scatter.10
  709.1 91.4 all-gather.4
where the time goes:
time: 850 us
  waiting for transfers between devices  495 us (58%)
  other arithmetic  200 us (24%)
  local copies, waits for them, and re-layouts  73.1 us (9%)
  blocking collectives  67.7 us (8%)
  between operations  14.3 us (2%)
    reduce_scatter x2, waiting for transfers between devices, level_update(): lax.psum_scatter(sums, 'item', scatter_dimension=1, tiled=True)  275 us
    all_gather x2, waiting for transfers between devices, level_update(): whole_new = lax.all_gather(own_new, 'item', axis=1, tiled=True)  138 us
    scatter-add x2, other arithmetic, level_update(): sums = jax.ops.segment_sum(columns.T, codes, num_segments=K).T  98 us
    scatter-add x2, other arithmetic, level_update(): jax.ops.segment_sum(jnp.ones(codes.shape, jnp.float32), codes, num_segmen...  86.6 us
    unnamed x8, waiting for transfers between devices  81.8 us
    psum x1, blocking collectives, on_device(): squares = lax.psum(jnp.sum(values * values, axis=0), 'code')  67.7 us
    gather x1, local copies, waits for them, and re-layouts, on_device(): leftover = middle - jnp.take(second_whole, second_codes, axis=1)  29.9 us
    gather x1, local copies, waits for them, and re-layouts, on_device(): middle = normed - jnp.take(first_whole, first_codes, axis=1)  29.9 us
  transfers between devices with their start and end apart: 6, of which 6 were waited for; matrix products, arithmetic and copies ran while one was open for 21% of the time, Pallas kernels for 0%

commit v1 on v0

v1 whole, which is shorter than its diff:
```python
import functools

import jax
import jax.numpy as jnp
from jax import lax
from jax.experimental import pallas as pl
from jax.experimental.pallas import tpu as pltpu
from jax.sharding import Mesh
from jax.sharding import PartitionSpec as P

D = 512
HI = 32
LO = 256
Y = 4
Z = 4
F = 16
PER = HI // Y
BLOCK = PER * F + PER
TILE = 2048
BF = jnp.bfloat16
F32 = jnp.float32
NT = (((1,), (1,)), ((), ()))


def split(v):
    top = v.astype(BF)
    return top, (v - top.astype(F32)).astype(BF)


def hi_lo(code):
    code = code.astype(jnp.int32)
    return (code >> 8).astype(F32).astype(BF), (code & (LO - 1)).astype(F32).astype(BF)


def rows_of(count, columns):
    return lax.broadcasted_iota(jnp.int32, (count, columns), 0).astype(F32).astype(BF)


def ones_where(mask):
    return jnp.where(mask, jnp.ones((), BF), jnp.zeros((), BF))


def one_hot(lo):
    return ones_where(lo == rows_of(LO, lo.shape[1]))


def masked(v, hi):
    zero = jnp.zeros((), BF)
    return [jnp.where(hi == jnp.array(h, BF), v, zero) for h in range(HI)]


def add_sums(values, code, init_ref, out_ref):
    hi, lo = hi_lo(code)
    top, rest = split(values)
    members = ones_where(hi == rows_of(HI, hi.shape[1]))
    left = jnp.concatenate(masked(top, hi) + masked(rest, hi) + [members], axis=0)
    s = lax.dot_general(left, one_hot(lo), NT, preferred_element_type=F32)
    half = HI * F
    sums = s[:half] + s[half : 2 * half]
    counts = s[2 * half :]

    @pl.when(pl.program_id(0) == 0)
    def _():
        out_ref[...] = jnp.zeros_like(out_ref) if init_ref is None else init_ref[...]

    for y in range(Y):
        out_ref[y, : PER * F, :] += sums[y * PER * F : (y + 1) * PER * F]
        out_ref[y, PER * F :, :] += counts[y * PER : (y + 1) * PER]


def looked_up(code, table_ref):
    hi, lo = hi_lo(code)
    hot = one_hot(lo)
    top, rest = split(table_ref[...])
    g = jnp.dot(top, hot, preferred_element_type=F32) + jnp.dot(rest, hot, preferred_element_type=F32)
    hi = hi.astype(F32)
    found = g[:F]
    for h in range(1, HI):
        found = jnp.where(hi == h, g[h * F : (h + 1) * F], found)
    return found


def first_kernel(with_init, values_ref, codes_ref, *refs):
    init_ref = refs[0] if with_init else None
    add_sums(values_ref[...], codes_ref[0:1], init_ref, refs[-1])


def second_kernel(with_init, values_ref, codes_ref, table_ref, *refs):
    init_ref = refs[0] if with_init else None
    middle_ref, out_ref = refs[-2:]
    middle = values_ref[...] - looked_up(codes_ref[0:1], table_ref)
    middle_ref[...] = middle
    add_sums(middle, codes_ref[1:2], init_ref, out_ref)


def last_kernel(middle_ref, codes_ref, table_ref, out_ref):
    out_ref[...] = middle_ref[...] - looked_up(codes_ref[1:2], table_ref)


def per_tile(rows, at=0):
    return pl.BlockSpec((rows, TILE), lambda i: (at, i))


def whole(*shape):
    return pl.BlockSpec(shape, lambda i: (0,) * len(shape))


SUMS = jax.ShapeDtypeStruct((Y, BLOCK, LO), F32)
PARAMS = pltpu.CompilerParams(vmem_limit_bytes=56 << 20)


def first_sums(packed, init=None):
    n = packed.shape[1]
    extra = [] if init is None else [init]
    return pl.pallas_call(
        functools.partial(first_kernel, init is not None),
        grid=(n // TILE,),
        in_specs=[per_tile(F), per_tile(8, F // 8)] + [whole(Y, BLOCK, LO)] * len(extra),
        out_specs=whole(Y, BLOCK, LO),
        out_shape=SUMS,
        compiler_params=PARAMS,
        name="first_sums",
    )(packed, packed, *extra)


def second_sums(packed, table, init=None):
    n = packed.shape[1]
    extra = [] if init is None else [init]
    return pl.pallas_call(
        functools.partial(second_kernel, init is not None),
        grid=(n // TILE,),
        in_specs=[per_tile(F), per_tile(8, F // 8), whole(HI * F, LO)] + [whole(Y, BLOCK, LO)] * len(extra),
        out_specs=(per_tile(F), whole(Y, BLOCK, LO)),
        out_shape=(jax.ShapeDtypeStruct((F, n), F32), SUMS),
        compiler_params=PARAMS,
        name="second_sums",
    )(packed, packed, table, *extra)


def last_lookup(middle, packed, table):
    n = middle.shape[1]
    return pl.pallas_call(
        last_kernel,
        grid=(n // TILE,),
        in_specs=[per_tile(F), per_tile(8, F // 8), whole(HI * F, LO)],
        out_specs=per_tile(F),
        out_shape=jax.ShapeDtypeStruct((F, n), F32),
        compiler_params=PARAMS,
        name="last_lookup",
    )(middle, packed, table)


def to_all(v, axis):
    return lax.all_to_all(jnp.broadcast_to(v[None], (4, *v.shape)), axis, 0, 0, tiled=True)


def swap_core(v):
    return lax.ppermute(v, "core", [(0, 1), (1, 0)])


def z_partners(first):
    steps = (1, 3) if first else (3, 1)
    return [(2 * z + c, 2 * (z ^ steps[c]) + c) for z in range(Z) for c in range(2)]


def updated(sums, old, core, zh):
    z_core = ("zh", "core")
    own = lax.all_to_all(sums, "y", 0, 0, tiled=True).sum(axis=0)
    olds = old.reshape(2 * F, LO)
    got = lax.ppermute(jnp.concatenate([own, olds]), z_core, z_partners(True))
    own = own + got[:BLOCK]
    olds = jnp.concatenate([olds, got[BLOCK:]])
    got = lax.ppermute(jnp.concatenate([own, olds]), z_core, z_partners(False))
    own = own + got[:BLOCK]
    olds = jnp.concatenate([olds, got[BLOCK:]]).reshape(Z, 2, F, LO)
    place = jnp.where(core == 0, jnp.array([0, 1, 3, 2]), jnp.array([0, 2, 3, 1]))
    olds = jnp.concatenate([lax.dynamic_slice_in_dim(olds, place[z ^ zh], 1) for z in range(Z)]).reshape(PER, F, LO)
    counts = own[PER * F :]
    new = 0.5 * olds + 0.5 * own[: PER * F].reshape(PER, F, LO) / (counts + 1.0)[:, None]
    return new, to_all(new, "y").reshape(HI * F, LO)


def on_device(e, first_codes, second_codes, first_old, second_old):
    core, zh = lax.axis_index("core"), lax.axis_index("zh")
    n = e.shape[1]
    values = e.astype(F32)
    squares = jnp.sum(values * values, axis=0)
    squares = to_all(squares, "x").sum(axis=0)
    squares = to_all(squares, "zl").sum(axis=0)
    normed = values * lax.rsqrt(squares / D + 1e-06)[None, :]
    codes = jnp.stack([first_codes, second_codes]).astype(F32)

    def packed(half):
        part = functools.partial(lax.dynamic_slice_in_dim, start_index=half * F, slice_size=F)
        olds = jnp.concatenate([part(first_old), part(second_old)]).reshape(1, n)
        return jnp.concatenate([part(normed), codes, olds, jnp.zeros((5, n), F32)])

    mine = packed(core)
    theirs = swap_core(packed(1 - core))

    def old_of(level):
        a, b = (v[F + 2].reshape(2, F, LO)[level] for v in (mine, theirs))
        return jnp.where(core == 0, jnp.stack([a, b]), jnp.stack([b, a]))

    sums = first_sums(theirs, first_sums(mine))
    first_block, first_table = updated(sums, old_of(0), core, zh)
    my_middle, sums = second_sums(mine, first_table)
    their_middle, sums = second_sums(theirs, first_table, sums)
    second_block, second_table = updated(sums, old_of(1), core, zh)
    their_rest = last_lookup(their_middle, theirs, second_table)

    def owned(block, at):
        return lax.dynamic_index_in_dim(block, 2 * zh + at, keepdims=False)

    tail = jnp.concatenate([owned(first_block, 1 - core), owned(second_block, 1 - core)]).reshape(1, n)
    got = swap_core(jnp.concatenate([their_rest, tail]))
    my_rest = last_lookup(my_middle, mine, second_table)
    got_new = got[F].reshape(2, F, LO)

    def joined(a, b):
        return jnp.where(core == 0, jnp.concatenate([a, b]), jnp.concatenate([b, a]))

    first_new = joined(owned(first_block, core), got_new[0])
    second_new = joined(owned(second_block, core), got_new[1])
    return first_new, second_new, joined(my_rest, got[:F])


def solution(mesh):
    grid = Mesh(mesh.devices.reshape(Y, Z, 2, 4, 4), ("y", "zh", "core", "zl", "x"))
    item, code = ("y", "zh", "core"), ("zl", "x")
    both = P(code, item)
    return jax.shard_map(
        on_device,
        mesh=grid,
        in_specs=(both, P(item), P(item), both, both),
        out_specs=(both, both, both),
        check_vma=False,
    )
```

time: 850 us -> 216 us (0.25)
  the two profiles are of different devices: /device:TPU:1 before, /device:TPU:3 now
where the time goes in v1:
time: 216 us; the launch traced here: 215 us
  waiting for transfers between devices  59.7 us (28%)
  Pallas kernels  57.4 us (27%)
  starting transfers between devices  56 us (26%)
  blocking collectives  19.8 us (9%)
  between operations  8.87 us (4%)
  local copies, waits for them, and re-layouts  6.65 us (3%)
  other arithmetic  6.4 us (3%)
    pallas_call x2, Pallas kernels, second_sums(): pl.pallas_call(functools.partial(second_kernel, init is not None), grid=(...  26.8 us
    ppermute x2, starting transfers between devices, swap_core(): return lax.ppermute(v, 'core', [(0, 1), (1, 0)])  19.9 us
    all_to_all x2, blocking collectives, to_all(): lax.all_to_all(jnp.broadcast_to(v[None], (4, *v.shape)), axis, 0, 0, tile...  19.8 us
    ppermute x2, waiting for transfers between devices, updated(): got = lax.ppermute(jnp.concatenate([own, olds]), z_core, z_partners(True))  19.4 us
    all_to_all x2, waiting for transfers between devices, updated(): own = lax.all_to_all(sums, 'y', 0, 0, tiled=True).sum(axis=0)  16.9 us
    pallas_call x2, Pallas kernels, first_sums(): pl.pallas_call(functools.partial(first_kernel, init is not None), grid=(n...  16.6 us
    pallas_call x2, Pallas kernels, last_lookup(): pl.pallas_call(last_kernel, grid=(n // TILE,), in_specs=[per_tile(F), per...  14 us
    ppermute x2, waiting for transfers between devices, updated(): got = lax.ppermute(jnp.concatenate([own, olds]), z_core, z_partners(False))  12.3 us
  transfers between devices with their start and end apart: 10, of which 8 were waited for; matrix products, arithmetic and copies ran while one was open for 1% of the time, Pallas kernels for 7%

profile of v1, /device:TPU:3, one launch (start us, length us, event | category | flops | bytes accessed | tf_op | source)
XLA Modules:
  0.0 215.0 jit_solution(15263843362524091007)
XLA Ops:
  1.9 7.7 %all_to_all.32 = f32[4,1,8192]{2,1,0:T(1,128)S(1)} all-to-all(f32[4,1,8192]{2,1,0:T(1,128)S(1)} %broadcast_in_dim.8), channel_id=1, replica_groups=mesh['y'=4,'zh'=4,'core'=2,'zl'=4,'x'=4] {'x'}, dimensions={0} | all-to-all | bytes 262144 | tf_op jit(solution)/shard_map/all_to_all | solution.py:154
  10.5 5.7 %all-to-all-start.1 = ((f32[4,1,8192]{2,1,0:T(1,128)}), f32[4,1,8192]{2,1,0:T(1,128)S(1)}, u32[]{:S(2)}, u32[]{:S(2)}) async-start(f32[4,1,8192]{2,1,0:T(1,128)} %broadcast_in_dim.9), calls=%async_computation.1 | async-start | bytes 262144 | tf_op jit(solution)/shard_map/all_to_all | solution.py:154
  16.6 4.5 %all-to-all-done.1 = f32[4,1,8192]{2,1,0:T(1,128)S(1)} async-done(((f32[4,1,8192]{2,1,0:T(1,128)}), f32[4,1,8192]{2,1,0:T(1,128)S(1)}, u32[]{:S(2)}, u32[]{:S(2)}) %all-to-all-start.1) | async-done | bytes 131104 | tf_op jit(solution)/shard_map/all_to_all | solution.py:154
  22.4 6.5 %collective-permute-start = (f32[24,8192]{1,0:T(8,128)S(1)}, f32[24,8192]{1,0:T(8,128)S(1)}, u32[]{:S(2)}, u32[]{:S(2)}) collective-permute-start(f32[24,8192]{1,0:T(8,128)S(1)} %get-tuple-element.30), channel_id=1, source_target_pairs={{0,16},{16,0},{1,17},{17,1},{2,18},{18,2},{3,19},{19,3},{4,20},{20... | collective-permute-start | bytes 2359304 | tf_op jit(solution)/shard_map/ppermute | solution.py:158
  28.9 8.2 %first_sums.2.refs_0_ = f32[4,136,256]{2,1,0:T(8,128)} custom-call(f32[24,8192]{1,0:T(8,128)} %get-tuple-element.29.values_ref.codes_ref, f32[24,8192]{1,0:T(8,128)} %get-tuple-element.29.values_ref.codes_ref), custom_call_target="tpu_custom_call" | custom-call | tf_op jit(solution)/shard_map/first_sums/pallas_call | solution.py:115
  38.0 8.4 %first_sums.3 = f32[4,136,256]{2,1,0:T(8,128)} custom-call(f32[24,8192]{1,0:T(8,128)} %copy-done, f32[24,8192]{1,0:T(8,128)} %copy-done, f32[4,136,256]{2,1,0:T(8,128)} %first_sums.2.refs_0_), custom_call_target="tpu_custom_call" | custom-call | tf_op jit(solution)/shard_map/first_sums/pallas_call | solution.py:115
  46.5 3.5 %all-to-all-start.2 = ((f32[4,136,256]{2,1,0:T(8,128)}), f32[4,136,256]{2,1,0:T(8,128)S(1)}, u32[]{:S(2)}, u32[]{:S(2)}) async-start(f32[4,136,256]{2,1,0:T(8,128)} %first_sums.3), calls=%async_computation.2 | async-start | bytes 1114112 | tf_op jit(solution)/shard_map/all_to_all | solution.py:168
  51.0 8.8 %all-to-all-done.2 = f32[4,136,256]{2,1,0:T(8,128)S(1)} async-done(((f32[4,136,256]{2,1,0:T(8,128)}), f32[4,136,256]{2,1,0:T(8,128)S(1)}, u32[]{:S(2)}, u32[]{:S(2)}) %all-to-all-start.2) | async-done | bytes 557088 | tf_op jit(solution)/shard_map/all_to_all | solution.py:168
  59.9 9.2 %collective-permute-start.1 = (f32[168,256]{1,0:T(8,128)S(1)}, f32[168,256]{1,0:T(8,128)S(1)}, u32[]{:S(2)}, u32[]{:S(2)}) collective-permute-start(f32[168,256]{1,0:T(8,128)S(1)} %pad_maximum_fusion.5), channel_id=1, source_target_pairs={{0,32},{16,112},{32,0},{48,80},{64,96},{80,48},{96,64},{112,16},{1... | collective-permute-start | bytes 516104 | tf_op jit(solution)/shard_map/ppermute | solution.py:170
  69.2 7.8 %collective-permute-done.1 = f32[168,256]{1,0:T(8,128)S(1)} collective-permute-done((f32[168,256]{1,0:T(8,128)S(1)}, f32[168,256]{1,0:T(8,128)S(1)}, u32[]{:S(2)}, u32[]{:S(2)}) %collective-permute-start.1) | collective-permute-done | bytes 172064 | tf_op jit(solution)/shard_map/ppermute | solution.py:170
  77.1 6.7 %collective-permute-start.2 = (f32[200,256]{1,0:T(8,128)S(1)}, f32[200,256]{1,0:T(8,128)S(1)}, u32[]{:S(2)}, u32[]{:S(2)}) collective-permute-start(f32[200,256]{1,0:T(8,128)S(1)} %pad_maximum_fusion.3), channel_id=1, source_target_pairs={{0,96},{16,48},{32,64},{48,16},{64,32},{80,112},{96,0},{112,80},{1... | collective-permute-start | bytes 614408 | tf_op jit(solution)/shard_map/ppermute | solution.py:173
  93.5 12.1 %all_to_all.33 = f32[4,8,16,256]{3,2,1,0:T(8,128)} all-to-all(f32[4,8,16,256]{3,2,1,0:T(8,128)S(1)} %broadcast_in_dim.10), channel_id=1, replica_groups=mesh['y'=4,'zh'=4,'core'=2,'zl'=4,'x'=4] {'y'}, dimensions={0} | all-to-all | bytes 1048576 | tf_op jit(solution)/shard_map/all_to_all | solution.py:154
  105.6 13.4 %second_sums.2 = (f32[16,8192]{1,0:T(8,128)}, f32[4,136,256]{2,1,0:T(8,128)}) custom-call(f32[24,8192]{1,0:T(8,128)} %get-tuple-element.29.values_ref.codes_ref, f32[24,8192]{1,0:T(8,128)} %get-tuple-element.29.values_ref.codes_ref, f32[512,256]{1,0:T(8,128)} %bitcast.42), custom_call_target="tpu_custom_call" | custom-call | tf_op jit(solution)/shard_map/second_sums/pallas_call | solution.py:129
  119.0 13.5 %second_sums.3 = (f32[16,8192]{1,0:T(8,128)}, f32[4,136,256]{2,1,0:T(8,128)}) custom-call(f32[24,8192]{1,0:T(8,128)} %copy-done, f32[24,8192]{1,0:T(8,128)} %copy-done, f32[512,256]{1,0:T(8,128)} %bitcast.43, f32[4,136,256]{2,1,0:T(8,128)} %get-tuple-element.7.refs_0_), custom_call_target="tpu_custom_call" | custom-call | tf_op jit(solution)/shard_map/second_sums/pallas_call | solution.py:129
  132.4 3.5 %all-to-all-start.4 = ((f32[4,136,256]{2,1,0:T(8,128)}), f32[4,136,256]{2,1,0:T(8,128)S(1)}, u32[]{:S(2)}, u32[]{:S(2)}) async-start(f32[4,136,256]{2,1,0:T(8,128)} %get-tuple-element.9), calls=%async_computation.4 | async-start | bytes 1114112 | tf_op jit(solution)/shard_map/all_to_all | solution.py:168
  135.9 8.1 %all-to-all-done.4 = f32[4,136,256]{2,1,0:T(8,128)S(1)} async-done(((f32[4,136,256]{2,1,0:T(8,128)}), f32[4,136,256]{2,1,0:T(8,128)S(1)}, u32[]{:S(2)}, u32[]{:S(2)}) %all-to-all-start.4) | async-done | bytes 557088 | tf_op jit(solution)/shard_map/all_to_all | solution.py:168
  144.1 1.9 collective-permute-start.3
  146.0 11.6 %collective-permute-done.3 = f32[168,256]{1,0:T(8,128)S(1)} collective-permute-done((f32[168,256]{1,0:T(8,128)S(1)}, f32[168,256]{1,0:T(8,128)S(1)}, u32[]{:S(2)}, u32[]{:S(2)}) %collective-permute-start.3) | collective-permute-done | bytes 172064 | tf_op jit(solution)/shard_map/ppermute | solution.py:170
  159.6 11.2 %collective-permute-done.4 = f32[200,256]{1,0:T(8,128)S(1)} collective-permute-done((f32[200,256]{1,0:T(8,128)S(1)}, f32[200,256]{1,0:T(8,128)S(1)}, u32[]{:S(2)}, u32[]{:S(2)}) %collective-permute-start.4) | collective-permute-done | bytes 204832 | tf_op jit(solution)/shard_map/ppermute | solution.py:173
  171.8 3.6 %all-to-all-start.5 = ((f32[4,8,16,256]{3,2,1,0:T(8,128)}), f32[4,8,16,256]{3,2,1,0:T(8,128)S(1)}, u32[]{:S(2)}, u32[]{:S(2)}) async-start(f32[4,8,16,256]{3,2,1,0:T(8,128)} %broadcast_in_dim.11), calls=%async_computation.5 | async-start | bytes 1048576 | tf_op jit(solution)/shard_map/all_to_all | solution.py:154
  175.6 6.6 %all-to-all-done.5 = f32[4,8,16,256]{3,2,1,0:T(8,128)S(1)} async-done(((f32[4,8,16,256]{3,2,1,0:T(8,128)}), f32[4,8,16,256]{3,2,1,0:T(8,128)S(1)}, u32[]{:S(2)}, u32[]{:S(2)}) %all-to-all-start.5) | async-done | bytes 524320 | tf_op jit(solution)/shard_map/all_to_all | solution.py:154
  183.0 7.0 %last_lookup.2 = f32[16,8192]{1,0:T(8,128)} custom-call(f32[16,8192]{1,0:T(8,128)} %get-tuple-element.8.middle_ref, f32[24,8192]{1,0:T(8,128)} %copy-done, f32[512,256]{1,0:T(8,128)} %bitcast.40), custom_call_target="tpu_custom_call" | custom-call | tf_op jit(solution)/shard_map/last_lookup/pallas_call | solution.py:142
  191.1 13.4 %collective-permute-start.5 = (f32[17,8192]{1,0:T(8,128)S(1)}, f32[17,8192]{1,0:T(8,128)S(1)}, u32[]{:S(2)}, u32[]{:S(2)}) collective-permute-start(f32[17,8192]{1,0:T(8,128)S(1)} %pad_maximum_fusion.2), channel_id=1, source_target_pairs={{0,16},{16,0},{1,17},{17,1},{2,18},{18,2},{3,19},{19,3},{4,20},{20... | collective-permute-start | bytes 1671176 | tf_op jit(solution)/shard_map/ppermute | solution.py:158
  204.5 7.0 %last_lookup.3 = f32[16,8192]{1,0:T(8,128)} custom-call(f32[16,8192]{1,0:T(8,128)} %get-tuple-element.10.middle_ref, f32[24,8192]{1,0:T(8,128)} %get-tuple-element.29.values_ref.codes_ref, f32[512,256]{1,0:T(8,128)} %bitcast.41), custom_call_target="tpu_custom_call" | custom-call | tf_op jit(solution)/shard_map/last_lookup/pallas_call | solution.py:142
  (88 shorter events, 16.1 us)
Async XLA Ops:
  9.8 6.5 %copy-start.4 = (s32[8192]{0:T(1024)S(1)}, s32[8192]{0:T(1024)}, u32[]{:S(2)}) copy-start(s32[8192]{0:T(1024)} %param.11) | copy-start | bytes 98308
  9.8 6.5 %copy-start.5 = (s32[8192]{0:T(1024)S(1)}, s32[8192]{0:T(1024)}, u32[]{:S(2)}) copy-start(s32[8192]{0:T(1024)} %param.10) | copy-start | bytes 98308
  9.8 6.6 %copy-start.6 = (f32[32,256]{1,0:T(8,128)S(1)}, f32[32,256]{1,0:T(8,128)}, u32[]{:S(2)}) copy-start(f32[32,256]{1,0:T(8,128)} %param.13) | copy-start | bytes 98308
  9.8 6.6 %copy-start.7 = (f32[32,256]{1,0:T(8,128)S(1)}, f32[32,256]{1,0:T(8,128)}, u32[]{:S(2)}) copy-start(f32[32,256]{1,0:T(8,128)} %param.12) | copy-start | bytes 98308
  10.5 10.7 %copy-start.2 = (bf16[32,8192]{1,0:T(8,128)(2,1)S(1)}, bf16[32,8192]{1,0:T(8,128)(2,1)}, u32[]{:S(2)}) copy-start(bf16[32,8192]{1,0:T(8,128)(2,1)} %param.9) | copy-start | bytes 1572868
  10.5 10.5 %all-to-all-start.1 = ((f32[4,1,8192]{2,1,0:T(1,128)}), f32[4,1,8192]{2,1,0:T(1,128)S(1)}, u32[]{:S(2)}, u32[]{:S(2)}) async-start(f32[4,1,8192]{2,1,0:T(1,128)} %broadcast_in_dim.9), calls=%async_computation.1 | async-start | bytes 262144 | tf_op jit(solution)/shard_map/all_to_all | solution.py:154
  22.4 14.7 %collective-permute-start = (f32[24,8192]{1,0:T(8,128)S(1)}, f32[24,8192]{1,0:T(8,128)S(1)}, u32[]{:S(2)}, u32[]{:S(2)}) collective-permute-start(f32[24,8192]{1,0:T(8,128)S(1)} %get-tuple-element.30), channel_id=1, source_target_pairs={{0,16},{16,0},{1,17},{17,1},{2,18},{18,2},{3,19},{19,3},{4,20},{20... | collective-permute-start | bytes 2359304 | tf_op jit(solution)/shard_map/ppermute | solution.py:158
  37.1 0.9 copy-start
  46.5 13.4 %all-to-all-start.2 = ((f32[4,136,256]{2,1,0:T(8,128)}), f32[4,136,256]{2,1,0:T(8,128)S(1)}, u32[]{:S(2)}, u32[]{:S(2)}) async-start(f32[4,136,256]{2,1,0:T(8,128)} %first_sums.3), calls=%async_computation.2 | async-start | bytes 1114112 | tf_op jit(solution)/shard_map/all_to_all | solution.py:168
  59.9 17.1 %collective-permute-start.1 = (f32[168,256]{1,0:T(8,128)S(1)}, f32[168,256]{1,0:T(8,128)S(1)}, u32[]{:S(2)}, u32[]{:S(2)}) collective-permute-start(f32[168,256]{1,0:T(8,128)S(1)} %pad_maximum_fusion.5), channel_id=1, source_target_pairs={{0,32},{16,112},{32,0},{48,80},{64,96},{80,48},{96,64},{112,16},{1... | collective-permute-start | bytes 516104 | tf_op jit(solution)/shard_map/ppermute | solution.py:170
  77.1 6.7 %copy-start.8 = (s32[4]{0:T(128)S(1)}, s32[4]{0:T(128)}, u32[]{:S(2)}) copy-start(s32[4]{0:T(128)} %constant.54.clone) | copy-start | bytes 52
  77.1 6.7 %copy-start.9 = (s32[4]{0:T(128)S(1)}, s32[4]{0:T(128)}, u32[]{:S(2)}) copy-start(s32[4]{0:T(128)} %constant.53.clone) | copy-start | bytes 52
  77.1 16.1 %collective-permute-start.2 = (f32[200,256]{1,0:T(8,128)S(1)}, f32[200,256]{1,0:T(8,128)S(1)}, u32[]{:S(2)}, u32[]{:S(2)}) collective-permute-start(f32[200,256]{1,0:T(8,128)S(1)} %pad_maximum_fusion.3), channel_id=1, source_target_pairs={{0,96},{16,48},{32,64},{48,16},{64,32},{80,112},{96,0},{112,80},{1... | collective-permute-start | bytes 614408 | tf_op jit(solution)/shard_map/ppermute | solution.py:173
  132.4 11.6 %all-to-all-start.4 = ((f32[4,136,256]{2,1,0:T(8,128)}), f32[4,136,256]{2,1,0:T(8,128)S(1)}, u32[]{:S(2)}, u32[]{:S(2)}) async-start(f32[4,136,256]{2,1,0:T(8,128)} %get-tuple-element.9), calls=%async_computation.4 | async-start | bytes 1114112 | tf_op jit(solution)/shard_map/all_to_all | solution.py:168
  144.1 13.5 %collective-permute-start.3 = (f32[168,256]{1,0:T(8,128)S(1)}, f32[168,256]{1,0:T(8,128)S(1)}, u32[]{:S(2)}, u32[]{:S(2)}) collective-permute-start(f32[168,256]{1,0:T(8,128)S(1)} %pad_maximum_fusion.6), channel_id=1, source_target_pairs={{0,32},{16,112},{32,0},{48,80},{64,96},{80,48},{96,64},{112,16},{1... | collective-permute-start | bytes 516104 | tf_op jit(solution)/shard_map/ppermute | solution.py:170
  157.7 13.1 %collective-permute-start.4 = (f32[200,256]{1,0:T(8,128)S(1)}, f32[200,256]{1,0:T(8,128)S(1)}, u32[]{:S(2)}, u32[]{:S(2)}) collective-permute-start(f32[200,256]{1,0:T(8,128)S(1)} %pad_maximum_fusion.4), channel_id=1, source_target_pairs={{0,96},{16,48},{32,64},{48,16},{64,32},{80,112},{96,0},{112,80},{1... | collective-permute-start | bytes 614408 | tf_op jit(solution)/shard_map/ppermute | solution.py:173
  171.8 10.4 %all-to-all-start.5 = ((f32[4,8,16,256]{3,2,1,0:T(8,128)}), f32[4,8,16,256]{3,2,1,0:T(8,128)S(1)}, u32[]{:S(2)}, u32[]{:S(2)}) async-start(f32[4,8,16,256]{3,2,1,0:T(8,128)} %broadcast_in_dim.11), calls=%async_computation.5 | async-start | bytes 1048576 | tf_op jit(solution)/shard_map/all_to_all | solution.py:154
  182.2 0.8 copy-start.1
  191.1 20.4 %collective-permute-start.5 = (f32[17,8192]{1,0:T(8,128)S(1)}, f32[17,8192]{1,0:T(8,128)S(1)}, u32[]{:S(2)}, u32[]{:S(2)}) collective-permute-start(f32[17,8192]{1,0:T(8,128)S(1)} %pad_maximum_fusion.2), channel_id=1, source_target_pairs={{0,16},{16,0},{1,17},{17,1},{2,18},{18,2},{3,19},{19,3},{4,20},{20... | collective-permute-start | bytes 1671176 | tf_op jit(solution)/shard_map/ppermute | solution.py:158
  211.6 1.0 copy-start.3

commit v2 on v0

v2 whole, which is shorter than its diff:
```python
import functools

import jax
import jax.numpy as jnp
from jax import lax
from jax.experimental import pallas as pl
from jax.experimental.pallas import tpu as pltpu
from jax.sharding import Mesh
from jax.sharding import PartitionSpec as P

D = 512
HI = 16
LO = 512
Y = 4
Z = 4
F = 16
SUM_ROWS = Z * F
BLOCK = SUM_ROWS + 8
TILE = 4096
CHUNK = 1024
BF = jnp.bfloat16
F32 = jnp.float32
NT = (((1,), (1,)), ((), ()))
PARTS = 1
WIDTH = LO // PARTS


def split(v):
    top = v.astype(BF)
    return top, (v - top.astype(F32)).astype(BF)


def hi_lo(code):
    code = code.astype(jnp.int32)
    return (code >> 9).astype(F32).astype(BF), (code & (LO - 1)).astype(F32)


def rows_of(count, columns):
    return lax.broadcasted_iota(jnp.int32, (count, columns), 0).astype(F32)


def ones_where(mask):
    return jnp.where(mask, jnp.ones((), BF), jnp.zeros((), BF))


def one_hot(lo):
    upper = jnp.where(lo >= 256, 1.0, 0.0)
    lower = (lo - 256 * upper).astype(BF)
    upper = upper.astype(BF)
    rows = rows_of(256, lo.shape[1]).astype(BF)
    none = jnp.array(-1, BF)
    return jnp.concatenate(
        [ones_where(jnp.where(upper == jnp.array(u, BF), lower, none) == rows) for u in range(2)], axis=0
    )


def masked(v, hi):
    zero = jnp.zeros((), BF)
    return [jnp.where(hi == jnp.array(h, BF), v, zero) for h in range(HI)]


def add_sums(values, hi, hot, out_refs):
    top, rest = split(values)
    members = ones_where(hi == rows_of(HI, hi.shape[1]).astype(BF))
    left = jnp.concatenate(masked(top, hi) + masked(rest, hi) + [members], axis=0)
    s = lax.dot_general(left, hot, NT, preferred_element_type=F32)
    half = HI * F
    sums = s[:half] + s[half : 2 * half]
    counts = s[2 * half :]
    for p, out_ref in enumerate(out_refs):
        columns = slice(p * WIDTH, (p + 1) * WIDTH)
        for y in range(Y):
            out_ref[y, :SUM_ROWS, :] += sums[y * SUM_ROWS : (y + 1) * SUM_ROWS, columns]
            out_ref[y, SUM_ROWS : SUM_ROWS + Z, :] += counts[y * Z : (y + 1) * Z, columns]


def looked_up(terms, hi, hot):
    g = jnp.dot(terms, jnp.concatenate([hot, hot], axis=0), preferred_element_type=F32)
    hi = hi.astype(F32)
    found = g[:F]
    for h in range(1, HI):
        found = jnp.where(hi == h, g[h * F : (h + 1) * F], found)
    return found


def terms_of(table_refs):
    tops, rests = zip(*(split(ref[...]) for ref in table_refs), strict=True)
    return jnp.concatenate([*tops, *rests], axis=1)


def chunks(body):
    for at in range(0, TILE, CHUNK):
        body(slice(at, at + CHUNK))


def squares_kernel(e_ref, out_ref):
    values = e_ref[...].astype(F32)
    total = jnp.sum(values * values, axis=0, keepdims=True)
    for at in range(out_ref.shape[0]):
        out_ref[at] = total


def first_kernel(with_init, values_ref, codes_ref, *refs):
    out_refs = refs[-PARTS:]

    @pl.when(pl.program_id(0) == 0)
    def _():
        for p, out_ref in enumerate(out_refs):
            out_ref[...] = refs[p][...] if with_init else jnp.zeros_like(out_ref)

    def body(at):
        hi, lo = hi_lo(codes_ref[0:1, at])
        add_sums(values_ref[:, at], hi, one_hot(lo), out_refs)

    chunks(body)


def second_kernel(tiles, mine_ref, my_codes_ref, theirs_ref, their_codes_ref, *refs):
    table_refs, middle_ref, out_refs = refs[:PARTS], refs[PARTS], refs[PARTS + 1 :]
    step = pl.program_id(0)
    terms = terms_of(table_refs)

    @pl.when(step == 0)
    def _():
        for out_ref in out_refs:
            out_ref[...] = jnp.zeros_like(out_ref)

    def body(at):
        values = jnp.where(step < tiles, mine_ref[:, at], theirs_ref[:, at])
        codes = jnp.where(step < tiles, my_codes_ref[0:2, at], their_codes_ref[0:2, at])
        hi, lo = hi_lo(codes[0:1])
        middle = values - looked_up(terms, hi, one_hot(lo))
        middle_ref[:, at] = middle
        hi, lo = hi_lo(codes[1:2])
        add_sums(middle, hi, one_hot(lo), out_refs)

    chunks(body)


def last_kernel(middle_ref, codes_ref, *refs):
    table_refs, out_ref = refs[:PARTS], refs[PARTS]
    terms = terms_of(table_refs)

    def body(at):
        hi, lo = hi_lo(codes_ref[1:2, at])
        out_ref[:, at] = middle_ref[:, at] - looked_up(terms, hi, one_hot(lo))

    chunks(body)


def whole(*shape):
    return pl.BlockSpec(shape, lambda *i: (0,) * len(shape))


def cost(products, columns):
    return pl.CostEstimate(flops=products * 4 * HI * F * LO * columns, bytes_accessed=8 * F * columns, transcendentals=0)


SUMS = [jax.ShapeDtypeStruct((Y, BLOCK, WIDTH), F32)] * PARTS
SUM_SPECS = [whole(Y, BLOCK, WIDTH)] * PARTS
TABLE_SPECS = [whole(HI * F, WIDTH)] * PARTS
PARAMS = pltpu.CompilerParams(vmem_limit_bytes=28 << 20)


def squares_of(e, copies):
    rows, n = e.shape
    return pl.pallas_call(
        squares_kernel,
        grid=(2,),
        in_specs=[pl.BlockSpec((rows, n // 2), lambda i: (0, i))],
        out_specs=pl.BlockSpec((copies, 1, n // 2), lambda i: (0, 0, i)),
        out_shape=jax.ShapeDtypeStruct((copies, 1, n), F32),
        compiler_params=PARAMS,
        name="squares",
    )(e)


def first_sums(packed, init=()):
    n = packed.shape[1]
    return pl.pallas_call(
        functools.partial(first_kernel, len(init) > 0),
        grid=(n // TILE,),
        in_specs=[pl.BlockSpec((F, TILE), lambda i: (0, i)), pl.BlockSpec((8, TILE), lambda i: (F // 8, i))]
        + SUM_SPECS[: len(init)],
        out_specs=SUM_SPECS,
        out_shape=SUMS,
        compiler_params=PARAMS,
        cost_estimate=cost(1, n),
        name="first_sums",
    )(packed, packed, *init)


def second_sums(mine, theirs, tables):
    n = mine.shape[1]
    tiles = n // TILE

    def early(i):
        return jnp.minimum(i, tiles - 1)

    def late(i):
        return jnp.maximum(i - tiles, 0)

    return pl.pallas_call(
        functools.partial(second_kernel, tiles),
        grid=(2 * tiles,),
        in_specs=[
            pl.BlockSpec((F, TILE), lambda i: (0, early(i))),
            pl.BlockSpec((8, TILE), lambda i: (F // 8, early(i))),
            pl.BlockSpec((F, TILE), lambda i: (0, late(i))),
            pl.BlockSpec((8, TILE), lambda i: (F // 8, late(i))),
            *TABLE_SPECS,
        ],
        out_specs=[pl.BlockSpec((F, TILE), lambda i: (0, i)), *SUM_SPECS],
        out_shape=[jax.ShapeDtypeStruct((F, 2 * n), F32), *SUMS],
        compiler_params=PARAMS,
        cost_estimate=cost(2, 2 * n),
        name="second_sums",
    )(mine, mine, theirs, theirs, *tables)


def last_lookup(middle, part, packed, tables):
    n = packed.shape[1]
    tiles = n // TILE
    return pl.pallas_call(
        last_kernel,
        grid=(tiles,),
        in_specs=[
            pl.BlockSpec((F, TILE), lambda i: (0, part * tiles + i)),
            pl.BlockSpec((8, TILE), lambda i: (F // 8, i)),
            *TABLE_SPECS,
        ],
        out_specs=pl.BlockSpec((F, TILE), lambda i: (0, i)),
        out_shape=jax.ShapeDtypeStruct((F, n), F32),
        compiler_params=PARAMS,
        cost_estimate=cost(1, n),
        name="last_lookup",
    )(middle, packed, *tables)


def to_all(v, axis, size=4):
    return lax.all_to_all(jnp.broadcast_to(v[None], (size, *v.shape)), axis, 0, 0, tiled=True)


def swap_core(v):
    return lax.ppermute(v, "core", [(0, 1), (1, 0)])


def swap_z(v, first):
    steps = (1, 3) if first else (3, 1)
    pairs = [(2 * z + c, 2 * (z ^ steps[c]) + c) for z in range(Z) for c in range(2)]
    return lax.ppermute(v, ("zh", "core"), pairs)


def at_y(parts):
    return [lax.all_to_all(part, "y", 0, 0, tiled=True).sum(axis=0) for part in parts]


def over_z(parts, first):
    return [part + swap_z(part, first) for part in parts]


def over_z_with(parts, old, core, zh):
    (own,) = parts
    got = swap_z(jnp.concatenate([own, old]), True)
    own, olds = own + got[:BLOCK], [old, got[BLOCK:]]
    got = swap_z(jnp.concatenate([own, *olds]), False)
    own, olds = own + got[:BLOCK], jnp.stack([*olds, got[BLOCK : BLOCK + F], got[BLOCK + F :]])
    near, far = jnp.where(core == 0, olds[1], olds[2]), jnp.where(core == 0, olds[2], olds[1])
    olds = jnp.stack([olds[0], near, olds[3], far])
    olds = jnp.where(zh % 2 == 0, olds, jnp.stack([olds[1], olds[0], olds[3], olds[2]]))
    olds = jnp.where(zh < 2, olds, jnp.concatenate([olds[2:], olds[:2]]))
    return [own], olds


def updated(parts, olds):
    news = []
    for p, own in enumerate(parts):
        counts = own[SUM_ROWS : SUM_ROWS + Z, None, :]
        old = olds[:, :, p * WIDTH : (p + 1) * WIDTH]
        news.append(0.5 * old + 0.5 * own[:SUM_ROWS].reshape(Z, F, WIDTH) / (counts + 1.0))
    return news


def tables_of(news):
    return [to_all(new, "y").reshape(HI * F, WIDTH) for new in news]


def on_device(e, first_codes, second_codes, first_old, second_old):
    core, zh = lax.axis_index("core"), lax.axis_index("zh")
    n = e.shape[1]

    def feature_half(v, which, axis):
        return lax.dynamic_slice_in_dim(v, which * F, F, axis)

    def by_core(mine, theirs, axis):
        return jnp.where(core == 0, jnp.concatenate([mine, theirs], axis), jnp.concatenate([theirs, mine], axis))

    def whole_columns(news):
        own = lax.dynamic_index_in_dim(jnp.concatenate(news, axis=2), zh, keepdims=False)
        first, last = own[:, :256], own[:, 256:]
        kept, sent = jnp.where(core == 0, first, last), jnp.where(core == 0, last, first)
        return kept, swap_core(sent)

    values = e.astype(F32)
    squares = lax.all_to_all(squares_of(e, 4), "x", 0, 0, tiled=True).reshape(4, n).sum(axis=0)
    squares = to_all(squares, "zl").sum(axis=0)
    normed = values * lax.rsqrt(squares / D + 1e-06)[None, :]
    codes = jnp.stack([first_codes, second_codes]).astype(F32)

    def packed(half):
        olds = jnp.stack([feature_half(first_old, half, 0), feature_half(second_old, half, 0)])
        return jnp.concatenate([feature_half(normed, half, 0), codes, olds.reshape(1, n), jnp.zeros((5, n), F32)])

    mine = packed(core)
    theirs = swap_core(packed(1 - core))

    sums = first_sums(theirs, first_sums(mine))
    olds = by_core(mine[F + 2].reshape(2, F, 256), theirs[F + 2].reshape(2, F, 256), 2)
    own, first_all = over_z_with(at_y(sums), olds[0], core, zh)
    first_news = updated(own, first_all)
    middle, *sums = second_sums(mine, theirs, tables_of(first_news))
    own = at_y(sums)
    own, first_news = lax.optimization_barrier((own, first_news))
    own, second_all = over_z_with(own, olds[1], core, zh)
    first_columns = whole_columns(first_news)
    own, first_new = lax.optimization_barrier((own, by_core(*first_columns, 0)))
    second_news = updated(own, second_all)
    second_columns = whole_columns(second_news)
    tables, second_new = lax.optimization_barrier((tables_of(second_news), by_core(*second_columns, 0)))
    their_rest = last_lookup(middle, 1, theirs, tables)
    got = swap_core(their_rest)
    my_rest = last_lookup(middle, 0, mine, tables)
    return first_new, second_new, by_core(my_rest, got, 0)


def solution(mesh):
    grid = Mesh(mesh.devices.reshape(Y, Z, 2, 4, 4), ("y", "zh", "core", "zl", "x"))
    item, code = ("y", "zh", "core"), ("zl", "x")
    both = P(code, item)
    return jax.shard_map(
        on_device,
        mesh=grid,
        in_specs=(both, P(item), P(item), both, both),
        out_specs=(both, both, both),
        check_vma=False,
    )
```

time: 850 us -> 189 us (0.22)
  waiting for transfers between devices: 495 us -> 48.2 us
  other arithmetic: 200 us -> 3.29 us
  local copies, waits for them, and re-layouts: 73.1 us -> 3.1 us
  starting transfers between devices: 0.25 us -> 56.9 us
  Pallas kernels: 0 us -> 39.9 us
  blocking collectives: 67.7 us -> 33.8 us
  between operations: 14.3 us -> 1.18 us
    reduce_scatter x2 -> x0, waiting for transfers between devices: 275 us -> none  [level_update(): lax.psum_scatter(sums, 'item', scatter_dimension=1, tiled=True)]
    scatter-add x4 -> x0, other arithmetic: 185 us -> none  [the longest x2 98 us: level_update(): sums = jax.ops.segment_sum(columns.T, codes, num_segments=K).T]
    all_gather x2 -> x0, waiting for transfers between devices: 138 us -> none  [level_update(): whole_new = lax.all_gather(own_new, 'item', axis=1, tiled=True)]
    unnamed x8 -> x0, waiting for transfers between devices: 81.8 us -> none
    psum x1 -> x0, blocking collectives: 67.7 us -> none  [on_device(): squares = lax.psum(jnp.sum(values * values, axis=0), 'code')]
    gather x2 -> x0, local copies, waits for them, and re-layouts: 59.8 us -> none  [the longest x1 29.9 us: on_device(): leftover = middle - jnp.take(second_whole, second_codes, axis=1)]
    ppermute x0 -> x8, starting transfers between devices: none -> 44.3 us  [the longest x4 23.4 us: swap_core(): return lax.ppermute(v, 'core', [(0, 1), (1, 0)])]
    pallas_call x0 -> x6, Pallas kernels: none -> 39.9 us  [the longest x1 19.1 us: second_sums(): pl.pallas_call(functools.partial(second_kernel, tiles), grid=(2 * tiles,)...]
  transfers between devices with their start and end apart: 6 -> 11, of which waited for: 6 -> 8; matrix products, arithmetic and copies ran while one was open for 21% -> 1% of each run, Pallas kernels for 0% -> 5%
where the time goes in v2:
time: 189 us; the launch traced here: 186 us
  starting transfers between devices  56.9 us (30%)
  waiting for transfers between devices  48.2 us (26%)
  Pallas kernels  39.9 us (21%)
  blocking collectives  33.8 us (18%)
  other arithmetic  3.29 us (2%)
  local copies, waits for them, and re-layouts  3.1 us (2%)
    ppermute x4, waiting for transfers between devices, swap_z(): return lax.ppermute(v, ('zh', 'core'), pairs)  32.1 us
    ppermute x4, starting transfers between devices, swap_core(): return lax.ppermute(v, 'core', [(0, 1), (1, 0)])  23.4 us
    ppermute x4, starting transfers between devices, swap_z(): return lax.ppermute(v, ('zh', 'core'), pairs)  20.8 us
    pallas_call x1, Pallas kernels, second_sums(): pl.pallas_call(functools.partial(second_kernel, tiles), grid=(2 * tiles,)...  19.1 us
    all_to_all x1, blocking collectives, to_all(): lax.all_to_all(jnp.broadcast_to(v[None], (size, *v.shape)), axis, 0, 0, t...  12.2 us
    all_to_all x1, blocking collectives, at_y(): lax.all_to_all(part, 'y', 0, 0, tiled=True).sum(axis=0)  12.1 us
    pallas_call x2, Pallas kernels, first_sums(): pl.pallas_call(functools.partial(first_kernel, len(init) > 0), grid=(n //...  10.9 us
    all_to_all x1, waiting for transfers between devices, at_y(): lax.all_to_all(part, 'y', 0, 0, tiled=True).sum(axis=0)  10.2 us
  transfers between devices with their start and end apart: 11, of which 8 were waited for; matrix products, arithmetic and copies ran while one was open for 1% of the time, Pallas kernels for 5%

profile of v2, /device:TPU:1, one launch (start us, length us, event | category | flops | bytes accessed | tf_op | source)
XLA Modules:
  0.0 186.4 jit_solution(12637586206418878283)
XLA Ops:
  1.9 9.5 %all_to_all.31 = f32[4,1,8192]{2,1,0:T(1,128)S(1)} all-to-all(f32[4,1,8192]{2,1,0:T(1,128)S(1)} %squares.1), channel_id=1, replica_groups=mesh['y'=4,'zh'=4,'core'=2,'zl'=4,'x'=4] {'x'}, dimensions={0} | all-to-all | bytes 262144 | tf_op jit(solution)/shard_map/all_to_all | solution.py:305
  12.3 5.7 %all-to-all-start.1 = ((f32[4,1,8192]{2,1,0:T(1,128)}), f32[4,1,8192]{2,1,0:T(1,128)S(1)}, u32[]{:S(2)}, u32[]{:S(2)}) async-start(f32[4,1,8192]{2,1,0:T(1,128)} %broadcast_in_dim.6), calls=%async_computation.1 | async-start | bytes 262144 | tf_op jit(solution)/shard_map/all_to_all | solution.py:241
  18.3 4.5 %all-to-all-done.1 = f32[4,1,8192]{2,1,0:T(1,128)S(1)} async-done(((f32[4,1,8192]{2,1,0:T(1,128)}), f32[4,1,8192]{2,1,0:T(1,128)S(1)}, u32[]{:S(2)}, u32[]{:S(2)}) %all-to-all-start.1) | async-done | bytes 131104 | tf_op jit(solution)/shard_map/all_to_all | solution.py:241
  23.3 6.5 %collective-permute-start = (f32[24,8192]{1,0:T(8,128)S(1)}, f32[24,8192]{1,0:T(8,128)S(1)}, u32[]{:S(2)}, u32[]{:S(2)}) collective-permute-start(f32[24,8192]{1,0:T(8,128)S(1)} %get-tuple-element.31), channel_id=1, source_target_pairs={{0,16},{16,0},{1,17},{17,1},{2,18},{18,2},{3,19},{19,3},{4,20},{20... | collective-permute-start | bytes 2359304 | tf_op jit(solution)/shard_map/ppermute | solution.py:245
  29.8 5.0 %first_sums.2.refs_0_ = f32[4,72,512]{2,1,0:T(8,128)S(1)} custom-call(f32[24,8192]{1,0:T(8,128)S(1)} %get-tuple-element.32.values_ref.codes_ref.mine_ref.my_codes_ref, f32[24,8192]{1,0:T(8,128)S(1)} %get-tuple-element.32.values_ref.codes_ref.mine_ref.my_codes_ref), custom_call_target="tpu_custom_call" | custom-call | flops 4294967296 | bytes 1048576 | tf_op jit(solution)/shard_map/first_sums/pallas_call | solution.py:180
  34.9 5.8 %first_sums.3 = f32[4,72,512]{2,1,0:T(8,128)} custom-call(f32[24,8192]{1,0:T(8,128)S(1)} %collective-permute-done.values_ref.codes_ref.theirs_ref.their_codes_ref, f32[24,8192]{1,0:T(8,128)S(1)} %collective-permute-done.values_ref.codes_ref.theirs_ref.their_codes_ref, f32[4,72,512]{2,1,0:T(8,128)S(1)} %first_sums.2.refs_0_), custom_call_target="tpu_custom_call" | custom-call | flops 4294967296 | bytes 1048576 | tf_op jit(solution)/shard_map/first_sums/pallas_call | solution.py:180
  40.7 3.5 %all-to-all-start.2 = ((f32[4,72,512]{2,1,0:T(8,128)}), f32[4,72,512]{2,1,0:T(8,128)S(1)}, u32[]{:S(2)}, u32[]{:S(2)}) async-start(f32[4,72,512]{2,1,0:T(8,128)} %first_sums.3), calls=%async_computation.2 | async-start | bytes 1179648 | tf_op jit(solution)/shard_map/all_to_all | solution.py:255
  44.4 10.2 %all-to-all-done.2 = f32[4,72,512]{2,1,0:T(8,128)S(1)} async-done(((f32[4,72,512]{2,1,0:T(8,128)}), f32[4,72,512]{2,1,0:T(8,128)S(1)}, u32[]{:S(2)}, u32[]{:S(2)}) %all-to-all-start.2) | async-done | bytes 589856 | tf_op jit(solution)/shard_map/all_to_all | solution.py:255
  54.6 9.2 %collective-permute-start.1 = (f32[88,512]{1,0:T(8,128)S(1)}, f32[88,512]{1,0:T(8,128)S(1)}, u32[]{:S(2)}, u32[]{:S(2)}) collective-permute-start(f32[88,512]{1,0:T(8,128)S(1)} %pad_maximum_fusion.4), channel_id=1, source_target_pairs={{0,32},{16,112},{32,0},{48,80},{64,96},{80,48},{96,64},{112,16},{1... | collective-permute-start | bytes 540680 | tf_op jit(solution)/shard_map/ppermute | solution.py:251
  63.8 8.2 %collective-permute-done.1 = f32[88,512]{1,0:T(8,128)S(1)} collective-permute-done((f32[88,512]{1,0:T(8,128)S(1)}, f32[88,512]{1,0:T(8,128)S(1)}, u32[]{:S(2)}, u32[]{:S(2)}) %collective-permute-start.1) | collective-permute-done | bytes 180256 | tf_op jit(solution)/shard_map/ppermute | solution.py:251
  72.1 6.7 %collective-permute-start.2 = (f32[104,512]{1,0:T(8,128)S(1)}, f32[104,512]{1,0:T(8,128)S(1)}, u32[]{:S(2)}, u32[]{:S(2)}) collective-permute-start(f32[104,512]{1,0:T(8,128)S(1)} %pad_maximum_fusion.2), channel_id=1, source_target_pairs={{0,96},{16,48},{32,64},{48,16},{64,32},{80,112},{96,0},{112,80},{1... | collective-permute-start | bytes 638984 | tf_op jit(solution)/shard_map/ppermute | solution.py:251
  78.8 9.6 %collective-permute-done.2 = f32[104,512]{1,0:T(8,128)S(1)} collective-permute-done((f32[104,512]{1,0:T(8,128)S(1)}, f32[104,512]{1,0:T(8,128)S(1)}, u32[]{:S(2)}, u32[]{:S(2)}) %collective-permute-start.2) | collective-permute-done | bytes 213024 | tf_op jit(solution)/shard_map/ppermute | solution.py:251
  88.7 12.2 %all_to_all.32 = f32[4,4,16,512]{3,2,1,0:T(8,128)S(1)} all-to-all(f32[4,4,16,512]{3,2,1,0:T(8,128)S(1)} %broadcast_in_dim.7), channel_id=1, replica_groups=mesh['y'=4,'zh'=4,'core'=2,'zl'=4,'x'=4] {'y'}, dimensions={0} | all-to-all | bytes 1048576 | tf_op jit(solution)/shard_map/all_to_all | solution.py:241
  100.9 19.1 %second_sums.1 = (f32[16,16384]{1,0:T(8,128)S(1)}, f32[4,72,512]{2,1,0:T(8,128)S(1)}) custom-call(f32[24,8192]{1,0:T(8,128)S(1)} %get-tuple-element.32.values_ref.codes_ref.mine_ref.my_codes_ref, f32[24,8192]{1,0:T(8,128)S(1)} %get-tuple-element.32.values_ref.codes_ref.mine_ref.my_codes_ref, ...), custom_call_target="tpu_custom_call" | custom-call | flops 17179869184 | bytes 2097152 | tf_op jit(solution)/shard_map/second_sums/pallas_call | solution.py:203
  120.0 12.1 %all_to_all.33 = f32[4,72,512]{2,1,0:T(8,128)S(1)} all-to-all(f32[4,72,512]{2,1,0:T(8,128)S(1)} %get-tuple-element.11), channel_id=1, replica_groups=mesh['y'=4,'zh'=4,'core'=2,'zl'=4,'x'=4] {'y'}, dimensions={0} | all-to-all | bytes 1179648 | tf_op jit(solution)/shard_map/all_to_all | solution.py:255
  134.1 11.5 %collective-permute-done.3 = f32[88,512]{1,0:T(8,128)S(1)} collective-permute-done((f32[88,512]{1,0:T(8,128)S(1)}, f32[88,512]{1,0:T(8,128)S(1)}, u32[]{:S(2)}, u32[]{:S(2)}) %collective-permute-start.3) | collective-permute-done | bytes 180256 | tf_op jit(solution)/shard_map/ppermute | solution.py:251
  145.7 3.0 %collective-permute-start.4 = (f32[104,512]{1,0:T(8,128)S(1)}, f32[104,512]{1,0:T(8,128)S(1)}, u32[]{:S(2)}, u32[]{:S(2)}) collective-permute-start(f32[104,512]{1,0:T(8,128)S(1)} %pad_maximum_fusion.3), channel_id=1, source_target_pairs={{0,96},{16,48},{32,64},{48,16},{64,32},{80,112},{96,0},{112,80},{1... | collective-permute-start | bytes 638984 | tf_op jit(solution)/shard_map/ppermute | solution.py:251
  148.8 3.6 %collective-permute-start.5 = (f32[16,256]{1,0:T(8,128)S(1)}, f32[16,256]{1,0:T(8,128)S(1)}, u32[]{:S(2)}, u32[]{:S(2)}) collective-permute-start(f32[16,256]{1,0:T(8,128)S(1)} %get-tuple-element.40), channel_id=1, source_target_pairs={{0,16},{16,0},{1,17},{17,1},{2,18},{18,2},{3,19},{19,3},{4,20},{20... | collective-permute-start | bytes 49160 | tf_op jit(solution)/shard_map/ppermute | solution.py:245
  153.8 2.7 %collective-permute-done.4 = f32[104,512]{1,0:T(8,128)S(1)} collective-permute-done((f32[104,512]{1,0:T(8,128)S(1)}, f32[104,512]{1,0:T(8,128)S(1)}, u32[]{:S(2)}, u32[]{:S(2)}) %collective-permute-start.4) | collective-permute-done | bytes 213024 | tf_op jit(solution)/shard_map/ppermute | solution.py:251
  157.6 3.5 %all-to-all-start.5 = ((f32[4,4,16,512]{3,2,1,0:T(8,128)}), f32[4,4,16,512]{3,2,1,0:T(8,128)S(1)}, u32[]{:S(2)}, u32[]{:S(2)}) async-start(f32[4,4,16,512]{3,2,1,0:T(8,128)} %broadcast_in_dim.8), calls=%async_computation.5 | async-start | bytes 1048576 | tf_op jit(solution)/shard_map/all_to_all | solution.py:241
  161.1 6.7 %collective-permute-start.6 = (f32[16,256]{1,0:T(8,128)S(1)}, f32[16,256]{1,0:T(8,128)S(1)}, u32[]{:S(2)}, u32[]{:S(2)}) collective-permute-start(f32[16,256]{1,0:T(8,128)S(1)} %get-tuple-element.38), channel_id=1, source_target_pairs={{0,16},{16,0},{1,17},{17,1},{2,18},{18,2},{3,19},{19,3},{4,20},{20... | collective-permute-start | bytes 49160 | tf_op jit(solution)/shard_map/ppermute | solution.py:245
  169.1 4.8 %last_lookup.3 = f32[16,8192]{1,0:T(8,128)S(1)} custom-call(f32[16,16384]{1,0:T(8,128)S(1)} %get-tuple-element.17.middle_ref, f32[24,8192]{1,0:T(8,128)S(1)} %collective-permute-done.values_ref.codes_ref.theirs_ref.their_codes_ref, f32[256,512]{1,0:T(8,128)S(1)} %bitcast.34), custom_call_target="tpu_custom_call" | custom-call | flops 4294967296 | bytes 1048576 | tf_op jit(solution)/shard_map/last_lookup/pallas_call | solution.py:224
  173.9 6.6 %collective-permute-start.7 = (f32[16,8192]{1,0:T(8,128)S(1)}, f32[16,8192]{1,0:T(8,128)S(1)}, u32[]{:S(2)}, u32[]{:S(2)}) collective-permute-start(f32[16,8192]{1,0:T(8,128)S(1)} %last_lookup.3), channel_id=1, source_target_pairs={{0,16},{16,0},{1,17},{17,1},{2,18},{18,2},{3,19},{19,3},{4,20},{20... | collective-permute-start | bytes 1572872 | tf_op jit(solution)/shard_map/ppermute | solution.py:245
  180.5 4.8 %last_lookup.2 = f32[16,8192]{1,0:T(8,128)S(1)} custom-call(f32[16,16384]{1,0:T(8,128)S(1)} %get-tuple-element.17.middle_ref, f32[24,8192]{1,0:T(8,128)S(1)} %get-tuple-element.32.values_ref.codes_ref.mine_ref.my_codes_ref, f32[256,512]{1,0:T(8,128)S(1)} %bitcast.35), custom_call_target="tpu_custom_call" | custom-call | flops 4294967296 | bytes 1048576 | tf_op jit(solution)/shard_map/last_lookup/pallas_call | solution.py:224
  (71 shorter events, 10.0 us)
Async XLA Ops:
  0.6 1.0 copy-start
  11.5 6.5 %copy-start.2 = (s32[8192]{0:T(1024)S(1)}, s32[8192]{0:T(1024)}, u32[]{:S(2)}) copy-start(s32[8192]{0:T(1024)} %param.7) | copy-start | bytes 98308
  11.5 6.5 %copy-start.3 = (s32[8192]{0:T(1024)S(1)}, s32[8192]{0:T(1024)}, u32[]{:S(2)}) copy-start(s32[8192]{0:T(1024)} %param.6) | copy-start | bytes 98308
  11.5 6.6 %copy-start.4 = (f32[32,256]{1,0:T(8,128)S(1)}, f32[32,256]{1,0:T(8,128)}, u32[]{:S(2)}) copy-start(f32[32,256]{1,0:T(8,128)} %param.9) | copy-start | bytes 98308
  11.5 6.6 %copy-start.5 = (f32[32,256]{1,0:T(8,128)S(1)}, f32[32,256]{1,0:T(8,128)}, u32[]{:S(2)}) copy-start(f32[32,256]{1,0:T(8,128)} %param.8) | copy-start | bytes 98308
  12.3 10.7 %copy-start.1 = (bf16[32,8192]{1,0:T(8,128)(2,1)S(1)}, bf16[32,8192]{1,0:T(8,128)(2,1)}, u32[]{:S(2)}) copy-start(bf16[32,8192]{1,0:T(8,128)(2,1)} %e_ref.1) | copy-start | bytes 1572868
  12.3 10.5 %all-to-all-start.1 = ((f32[4,1,8192]{2,1,0:T(1,128)}), f32[4,1,8192]{2,1,0:T(1,128)S(1)}, u32[]{:S(2)}, u32[]{:S(2)}) async-start(f32[4,1,8192]{2,1,0:T(1,128)} %broadcast_in_dim.6), calls=%async_computation.1 | async-start | bytes 262144 | tf_op jit(solution)/shard_map/all_to_all | solution.py:241
  23.3 11.6 %collective-permute-start = (f32[24,8192]{1,0:T(8,128)S(1)}, f32[24,8192]{1,0:T(8,128)S(1)}, u32[]{:S(2)}, u32[]{:S(2)}) collective-permute-start(f32[24,8192]{1,0:T(8,128)S(1)} %get-tuple-element.31), channel_id=1, source_target_pairs={{0,16},{16,0},{1,17},{17,1},{2,18},{18,2},{3,19},{19,3},{4,20},{20... | collective-permute-start | bytes 2359304 | tf_op jit(solution)/shard_map/ppermute | solution.py:245
  40.7 13.8 %all-to-all-start.2 = ((f32[4,72,512]{2,1,0:T(8,128)}), f32[4,72,512]{2,1,0:T(8,128)S(1)}, u32[]{:S(2)}, u32[]{:S(2)}) async-start(f32[4,72,512]{2,1,0:T(8,128)} %first_sums.3), calls=%async_computation.2 | async-start | bytes 1179648 | tf_op jit(solution)/shard_map/all_to_all | solution.py:255
  54.6 17.4 %collective-permute-start.1 = (f32[88,512]{1,0:T(8,128)S(1)}, f32[88,512]{1,0:T(8,128)S(1)}, u32[]{:S(2)}, u32[]{:S(2)}) collective-permute-start(f32[88,512]{1,0:T(8,128)S(1)} %pad_maximum_fusion.4), channel_id=1, source_target_pairs={{0,32},{16,112},{32,0},{48,80},{64,96},{80,48},{96,64},{112,16},{1... | collective-permute-start | bytes 540680 | tf_op jit(solution)/shard_map/ppermute | solution.py:251
  72.1 16.4 %collective-permute-start.2 = (f32[104,512]{1,0:T(8,128)S(1)}, f32[104,512]{1,0:T(8,128)S(1)}, u32[]{:S(2)}, u32[]{:S(2)}) collective-permute-start(f32[104,512]{1,0:T(8,128)S(1)} %pad_maximum_fusion.2), channel_id=1, source_target_pairs={{0,96},{16,48},{32,64},{48,16},{64,32},{80,112},{96,0},{112,80},{1... | collective-permute-start | bytes 638984 | tf_op jit(solution)/shard_map/ppermute | solution.py:251
  132.2 13.5 %collective-permute-start.3 = (f32[88,512]{1,0:T(8,128)S(1)}, f32[88,512]{1,0:T(8,128)S(1)}, u32[]{:S(2)}, u32[]{:S(2)}) collective-permute-start(f32[88,512]{1,0:T(8,128)S(1)} %pad_maximum_fusion.5), channel_id=1, source_target_pairs={{0,32},{16,112},{32,0},{48,80},{64,96},{80,48},{96,64},{112,16},{1... | collective-permute-start | bytes 540680 | tf_op jit(solution)/shard_map/ppermute | solution.py:251
  145.7 10.8 %collective-permute-start.4 = (f32[104,512]{1,0:T(8,128)S(1)}, f32[104,512]{1,0:T(8,128)S(1)}, u32[]{:S(2)}, u32[]{:S(2)}) collective-permute-start(f32[104,512]{1,0:T(8,128)S(1)} %pad_maximum_fusion.3), channel_id=1, source_target_pairs={{0,96},{16,48},{32,64},{48,16},{64,32},{80,112},{96,0},{112,80},{1... | collective-permute-start | bytes 638984 | tf_op jit(solution)/shard_map/ppermute | solution.py:251
  148.8 4.4 %collective-permute-start.5 = (f32[16,256]{1,0:T(8,128)S(1)}, f32[16,256]{1,0:T(8,128)S(1)}, u32[]{:S(2)}, u32[]{:S(2)}) collective-permute-start(f32[16,256]{1,0:T(8,128)S(1)} %get-tuple-element.40), channel_id=1, source_target_pairs={{0,16},{16,0},{1,17},{17,1},{2,18},{18,2},{3,19},{19,3},{4,20},{20... | collective-permute-start | bytes 49160 | tf_op jit(solution)/shard_map/ppermute | solution.py:245
  157.6 11.5 %all-to-all-start.5 = ((f32[4,4,16,512]{3,2,1,0:T(8,128)}), f32[4,4,16,512]{3,2,1,0:T(8,128)S(1)}, u32[]{:S(2)}, u32[]{:S(2)}) async-start(f32[4,4,16,512]{3,2,1,0:T(8,128)} %broadcast_in_dim.8), calls=%async_computation.5 | async-start | bytes 1048576 | tf_op jit(solution)/shard_map/all_to_all | solution.py:241
  161.1 7.4 %collective-permute-start.6 = (f32[16,256]{1,0:T(8,128)S(1)}, f32[16,256]{1,0:T(8,128)S(1)}, u32[]{:S(2)}, u32[]{:S(2)}) collective-permute-start(f32[16,256]{1,0:T(8,128)S(1)} %get-tuple-element.38), channel_id=1, source_target_pairs={{0,16},{16,0},{1,17},{17,1},{2,18},{18,2},{3,19},{19,3},{4,20},{20... | collective-permute-start | bytes 49160 | tf_op jit(solution)/shard_map/ppermute | solution.py:245
  173.9 11.4 %collective-permute-start.7 = (f32[16,8192]{1,0:T(8,128)S(1)}, f32[16,8192]{1,0:T(8,128)S(1)}, u32[]{:S(2)}, u32[]{:S(2)}) collective-permute-start(f32[16,8192]{1,0:T(8,128)S(1)} %last_lookup.3), channel_id=1, source_target_pairs={{0,16},{16,0},{1,17},{17,1},{2,18},{18,2},{3,19},{19,3},{4,20},{20... | collective-permute-start | bytes 1572872 | tf_op jit(solution)/shard_map/ppermute | solution.py:245

commit v3 on v2

--- a/solution.py
+++ b/solution.py
@@ -17,8 +17,10 @@
 SUM_ROWS = Z * F
 BLOCK = SUM_ROWS + 8
 TILE = 4096
-CHUNK = 1024
+CHUNK = 4096
 BF = jnp.bfloat16
+F8 = jnp.float8_e4m3fn
+REST_MAX = 256.0
 F32 = jnp.float32
 NT = (((1,), (1,)), ((), ()))
 PARTS = 1
@@ -27,7 +29,9 @@
 
 def split(v):
     top = v.astype(BF)
-    return top, (v - top.astype(F32)).astype(BF)
+    largest = jnp.maximum(jnp.max(jnp.abs(v), keepdims=True), 1e-30)
+    scale = (REST_MAX * 256.0) / largest
+    return top, (v - top.astype(F32)) * scale, largest * (1.0 / (REST_MAX * 256.0))
 
 
 def hi_lo(code):
@@ -60,13 +64,14 @@
 
 
 def add_sums(values, hi, hot, out_refs):
-    top, rest = split(values)
+    top, rest, unscale = split(values)
     members = ones_where(hi == rows_of(HI, hi.shape[1]).astype(BF))
-    left = jnp.concatenate(masked(top, hi) + masked(rest, hi) + [members], axis=0)
+    left = jnp.concatenate(masked(top, hi) + [members], axis=0)
     s = lax.dot_general(left, hot, NT, preferred_element_type=F32)
-    half = HI * F
-    sums = s[:half] + s[half : 2 * half]
-    counts = s[2 * half :]
+    left = jnp.concatenate(masked(rest.astype(BF), hi), axis=0).astype(F8)
+    fine = lax.dot_general(left, hot.astype(F8), NT, preferred_element_type=F32)
+    sums = s[: HI * F] + fine * unscale
+    counts = s[HI * F :]
     for p, out_ref in enumerate(out_refs):
         columns = slice(p * WIDTH, (p + 1) * WIDTH)
         for y in range(Y):
@@ -84,8 +89,9 @@
 
 
 def terms_of(table_refs):
-    tops, rests = zip(*(split(ref[...]) for ref in table_refs), strict=True)
-    return jnp.concatenate([*tops, *rests], axis=1)
+    v = jnp.concatenate([ref[...] for ref in table_refs], axis=1)
+    top = v.astype(BF)
+    return jnp.concatenate([top, (v - top.astype(F32)).astype(BF)], axis=1)
 
 
 def chunks(body):
@@ -138,14 +144,16 @@
 
 
 def last_kernel(middle_ref, codes_ref, *refs):
-    table_refs, out_ref = refs[:PARTS], refs[PARTS]
+    table_refs, tail_refs, out_ref = refs[:PARTS], refs[PARTS:-1], refs[-1]
     terms = terms_of(table_refs)
 
     def body(at):
         hi, lo = hi_lo(codes_ref[1:2, at])
-        out_ref[:, at] = middle_ref[:, at] - looked_up(terms, hi, one_hot(lo))
+        out_ref[:F, at] = middle_ref[:, at] - looked_up(terms, hi, one_hot(lo))
 
     chunks(body)
+    for ref in tail_refs:
+        out_ref[F:, :] = ref[...]
 
 
 def whole(*shape):
@@ -159,7 +167,7 @@
 SUMS = [jax.ShapeDtypeStruct((Y, BLOCK, WIDTH), F32)] * PARTS
 SUM_SPECS = [whole(Y, BLOCK, WIDTH)] * PARTS
 TABLE_SPECS = [whole(HI * F, WIDTH)] * PARTS
-PARAMS = pltpu.CompilerParams(vmem_limit_bytes=28 << 20)
+PARAMS = pltpu.CompilerParams(vmem_limit_bytes=32 << 20)
 
 
 def squares_of(e, copies):
@@ -218,8 +226,9 @@
     )(mine, mine, theirs, theirs, *tables)
 
 
-def last_lookup(middle, part, packed, tables):
+def last_lookup(middle, part, packed, tables, tail=()):
     n = packed.shape[1]
+    rows = F + 8 * len(tail)
     tiles = n // TILE
     return pl.pallas_call(
         last_kernel,
@@ -228,13 +237,14 @@
             pl.BlockSpec((F, TILE), lambda i: (0, part * tiles + i)),
             pl.BlockSpec((8, TILE), lambda i: (F // 8, i)),
             *TABLE_SPECS,
-        ],
-        out_specs=pl.BlockSpec((F, TILE), lambda i: (0, i)),
-        out_shape=jax.ShapeDtypeStruct((F, n), F32),
+        ]
+        + [pl.BlockSpec((8, TILE), lambda i: (0, i))] * len(tail),
+        out_specs=pl.BlockSpec((rows, TILE), lambda i: (0, i)),
+        out_shape=jax.ShapeDtypeStruct((rows, n), F32),
         compiler_params=PARAMS,
         cost_estimate=cost(1, n),
         name="last_lookup",
-    )(middle, packed, *tables)
+    )(middle, packed, *tables, *tail)
 
 
 def to_all(v, axis, size=4):
@@ -295,11 +305,10 @@
     def by_core(mine, theirs, axis):
         return jnp.where(core == 0, jnp.concatenate([mine, theirs], axis), jnp.concatenate([theirs, mine], axis))
 
-    def whole_columns(news):
+    def owned(news):
         own = lax.dynamic_index_in_dim(jnp.concatenate(news, axis=2), zh, keepdims=False)
         first, last = own[:, :256], own[:, 256:]
-        kept, sent = jnp.where(core == 0, first, last), jnp.where(core == 0, last, first)
-        return kept, swap_core(sent)
+        return jnp.where(core == 0, first, last), jnp.where(core == 0, last, first)
 
     values = e.astype(F32)
     squares = lax.all_to_all(squares_of(e, 4), "x", 0, 0, tiled=True).reshape(4, n).sum(axis=0)
@@ -316,21 +325,23 @@
 
     sums = first_sums(theirs, first_sums(mine))
     olds = by_core(mine[F + 2].reshape(2, F, 256), theirs[F + 2].reshape(2, F, 256), 2)
-    own, first_all = over_z_with(at_y(sums), olds[0], core, zh)
-    first_news = updated(own, first_all)
+    own, old = over_z_with(at_y(sums), olds[0], core, zh)
+    first_news = updated(own, old)
+
     middle, *sums = second_sums(mine, theirs, tables_of(first_news))
-    own = at_y(sums)
-    own, first_news = lax.optimization_barrier((own, first_news))
-    own, second_all = over_z_with(own, olds[1], core, zh)
-    first_columns = whole_columns(first_news)
-    own, first_new = lax.optimization_barrier((own, by_core(*first_columns, 0)))
-    second_news = updated(own, second_all)
-    second_columns = whole_columns(second_news)
-    tables, second_new = lax.optimization_barrier((tables_of(second_news), by_core(*second_columns, 0)))
-    their_rest = last_lookup(middle, 1, theirs, tables)
-    got = swap_core(their_rest)
-    my_rest = last_lookup(middle, 0, mine, tables)
-    return first_new, second_new, by_core(my_rest, got, 0)
+    own, first_news = lax.optimization_barrier((at_y(sums), first_news))
+    own, old = over_z_with(own, olds[1], core, zh)
+    kept, sent = owned(first_news)
+    own, first_new = lax.optimization_barrier((own, by_core(kept, swap_core(sent), 0)))
+    second_news = updated(own, old)
+
+    tables, second_news = lax.optimization_barrier((tables_of(second_news), second_news))
+    kept, sent = owned(second_news)
+    tail = jnp.concatenate([sent.reshape(1, -1), jnp.zeros((1, n - sent.size), F32)], axis=1)
+    got = swap_core(last_lookup(middle, 1, theirs, tables, [jnp.broadcast_to(tail, (8, n))]))
+    rest = last_lookup(middle, 0, mine, tables)
+    second_new = by_core(kept, got[F, : sent.size].reshape(sent.shape), 0)
+    return first_new, second_new, by_core(rest, got[:F], 0)
 
 
 def solution(mesh):

time: 189 us -> 189 us (level); the launches traced: 186 us -> 189 us
  blocking collectives: 33.8 us -> 40.4 us
  waiting for transfers between devices: 48.2 us -> 41.7 us
  starting transfers between devices: 56.9 us -> 62.9 us
  Pallas kernels: 39.9 us -> 36.8 us
    all_to_all x1 -> x2, blocking collectives: 12.2 us -> 20.3 us  [to_all(): lax.all_to_all(jnp.broadcast_to(v[None], (size, *v.shape)), axis, 0, 0, t...]
    ppermute x4, waiting for transfers between devices: 32.1 us -> 26.2 us  [swap_z(): return lax.ppermute(v, ('zh', 'core'), pairs)]
    ppermute x4, starting transfers between devices: 20.8 us -> 26.3 us  [swap_z(): return lax.ppermute(v, ('zh', 'core'), pairs)]
    ppermute x4 -> x3, starting transfers between devices: 23.4 us -> 27.4 us  [swap_core(): return lax.ppermute(v, 'core', [(0, 1), (1, 0)])]
    all_to_all x2 -> x1, starting transfers between devices: 9.22 us -> 5.75 us  [to_all(): lax.all_to_all(jnp.broadcast_to(v[None], (size, *v.shape)), axis, 0, 0, t...]
    all_to_all x2 -> x1, waiting for transfers between devices: 4.46 us -> 4.46 us  [to_all(): lax.all_to_all(jnp.broadcast_to(v[None], (size, *v.shape)), axis, 0, 0, t...]
  transfers between devices with their start and end apart: 11 -> 9, of which waited for: 8 -> 6; matrix products, arithmetic and copies ran while one was open for 1% -> 1% of each run, Pallas kernels for 5% -> 5%
where the time goes in v3:
time: 189 us
  starting transfers between devices  62.9 us (33%)
  waiting for transfers between devices  41.7 us (22%)
  blocking collectives  40.4 us (21%)
  Pallas kernels  36.8 us (19%)
  other arithmetic  3.3 us (2%)
  local copies, waits for them, and re-layouts  2.43 us (1%)
    ppermute x3, starting transfers between devices, swap_core(): return lax.ppermute(v, 'core', [(0, 1), (1, 0)])  27.4 us
    ppermute x4, starting transfers between devices, swap_z(): return lax.ppermute(v, ('zh', 'core'), pairs)  26.3 us
    ppermute x4, waiting for transfers between devices, swap_z(): return lax.ppermute(v, ('zh', 'core'), pairs)  26.2 us
    all_to_all x2, blocking collectives, to_all(): lax.all_to_all(jnp.broadcast_to(v[None], (size, *v.shape)), axis, 0, 0, t...  20.3 us
    pallas_call x1, Pallas kernels, second_sums(): pl.pallas_call(functools.partial(second_kernel, tiles), grid=(2 * tiles,)...  17.6 us
    all_to_all x1, blocking collectives, at_y(): lax.all_to_all(part, 'y', 0, 0, tiled=True).sum(axis=0)  10.6 us
    all_to_all x1, waiting for transfers between devices, at_y(): lax.all_to_all(part, 'y', 0, 0, tiled=True).sum(axis=0)  10.2 us
    pallas_call x2, Pallas kernels, last_lookup(): pl.pallas_call(last_kernel, grid=(tiles,), in_specs=[pl.BlockSpec((F, TIL...  9.7 us
  transfers between devices with their start and end apart: 9, of which 6 were waited for; matrix products, arithmetic and copies ran while one was open for 1% of the time, Pallas kernels for 5%

profile of v3, /device:TPU:1, one launch (start us, length us, event | category | flops | bytes accessed | tf_op | source)
XLA Modules:
  0.0 188.6 jit_solution(271149180879232185)
XLA Ops:
  1.9 9.5 %all_to_all.31 = f32[4,1,8192]{2,1,0:T(1,128)S(1)} all-to-all(f32[4,1,8192]{2,1,0:T(1,128)S(1)} %squares.1), channel_id=1, replica_groups=mesh['y'=4,'zh'=4,'core'=2,'zl'=4,'x'=4] {'x'}, dimensions={0} | all-to-all | bytes 262144 | tf_op jit(solution)/shard_map/all_to_all | solution.py:314
  12.3 5.7 %all-to-all-start.1 = ((f32[4,1,8192]{2,1,0:T(1,128)}), f32[4,1,8192]{2,1,0:T(1,128)S(1)}, u32[]{:S(2)}, u32[]{:S(2)}) async-start(f32[4,1,8192]{2,1,0:T(1,128)} %broadcast_in_dim.10), calls=%async_computation.1 | async-start | bytes 262144 | tf_op jit(solution)/shard_map/all_to_all | solution.py:251
  18.3 4.5 %all-to-all-done.1 = f32[4,1,8192]{2,1,0:T(1,128)S(1)} async-done(((f32[4,1,8192]{2,1,0:T(1,128)}), f32[4,1,8192]{2,1,0:T(1,128)S(1)}, u32[]{:S(2)}, u32[]{:S(2)}) %all-to-all-start.1) | async-done | bytes 131104 | tf_op jit(solution)/shard_map/all_to_all | solution.py:251
  23.3 6.5 %collective-permute-start = (f32[24,8192]{1,0:T(8,128)S(1)}, f32[24,8192]{1,0:T(8,128)S(1)}, u32[]{:S(2)}, u32[]{:S(2)}) collective-permute-start(f32[24,8192]{1,0:T(8,128)S(1)} %get-tuple-element.31), channel_id=1, source_target_pairs={{0,16},{16,0},{1,17},{17,1},{2,18},{18,2},{3,19},{19,3},{4,20},{20... | collective-permute-start | bytes 2359304 | tf_op jit(solution)/shard_map/ppermute | solution.py:255
  29.8 4.2 %first_sums.2.refs_0_ = f32[4,72,512]{2,1,0:T(8,128)S(1)} custom-call(f32[24,8192]{1,0:T(8,128)S(1)} %get-tuple-element.32.values_ref.codes_ref.mine_ref.my_codes_ref, f32[24,8192]{1,0:T(8,128)S(1)} %get-tuple-element.32.values_ref.codes_ref.mine_ref.my_codes_ref), custom_call_target="tpu_custom_call" | custom-call | flops 4294967296 | bytes 1048576 | tf_op jit(solution)/shard_map/first_sums/pallas_call | solution.py:188
  34.1 5.0 %first_sums.3 = f32[4,72,512]{2,1,0:T(8,128)} custom-call(f32[24,8192]{1,0:T(8,128)S(1)} %collective-permute-done.values_ref.codes_ref.theirs_ref.their_codes_ref, f32[24,8192]{1,0:T(8,128)S(1)} %collective-permute-done.values_ref.codes_ref.theirs_ref.their_codes_ref, f32[4,72,512]{2,1,0:T(8,128)S(1)} %first_sums.2.refs_0_), custom_call_target="tpu_custom_call" | custom-call | flops 4294967296 | bytes 1048576 | tf_op jit(solution)/shard_map/first_sums/pallas_call | solution.py:188
  39.1 3.5 %all-to-all-start.2 = ((f32[4,72,512]{2,1,0:T(8,128)}), f32[4,72,512]{2,1,0:T(8,128)S(1)}, u32[]{:S(2)}, u32[]{:S(2)}) async-start(f32[4,72,512]{2,1,0:T(8,128)} %first_sums.3), calls=%async_computation.2 | async-start | bytes 1179648 | tf_op jit(solution)/shard_map/all_to_all | solution.py:265
  42.7 10.2 %all-to-all-done.2 = f32[4,72,512]{2,1,0:T(8,128)S(1)} async-done(((f32[4,72,512]{2,1,0:T(8,128)}), f32[4,72,512]{2,1,0:T(8,128)S(1)}, u32[]{:S(2)}, u32[]{:S(2)}) %all-to-all-start.2) | async-done | bytes 589856 | tf_op jit(solution)/shard_map/all_to_all | solution.py:265
  53.0 9.2 %collective-permute-start.1 = (f32[88,512]{1,0:T(8,128)S(1)}, f32[88,512]{1,0:T(8,128)S(1)}, u32[]{:S(2)}, u32[]{:S(2)}) collective-permute-start(f32[88,512]{1,0:T(8,128)S(1)} %pad_maximum_fusion.4), channel_id=1, source_target_pairs={{0,32},{16,112},{32,0},{48,80},{64,96},{80,48},{96,64},{112,16},{1... | collective-permute-start | bytes 540680 | tf_op jit(solution)/shard_map/ppermute | solution.py:261
  62.2 8.2 %collective-permute-done.1 = f32[88,512]{1,0:T(8,128)S(1)} collective-permute-done((f32[88,512]{1,0:T(8,128)S(1)}, f32[88,512]{1,0:T(8,128)S(1)}, u32[]{:S(2)}, u32[]{:S(2)}) %collective-permute-start.1) | collective-permute-done | bytes 180256 | tf_op jit(solution)/shard_map/ppermute | solution.py:261
  70.4 6.7 %collective-permute-start.2 = (f32[104,512]{1,0:T(8,128)S(1)}, f32[104,512]{1,0:T(8,128)S(1)}, u32[]{:S(2)}, u32[]{:S(2)}) collective-permute-start(f32[104,512]{1,0:T(8,128)S(1)} %pad_maximum_fusion.2), channel_id=1, source_target_pairs={{0,96},{16,48},{32,64},{48,16},{64,32},{80,112},{96,0},{112,80},{1... | collective-permute-start | bytes 638984 | tf_op jit(solution)/shard_map/ppermute | solution.py:261
  77.1 9.8 %collective-permute-done.2 = f32[104,512]{1,0:T(8,128)S(1)} collective-permute-done((f32[104,512]{1,0:T(8,128)S(1)}, f32[104,512]{1,0:T(8,128)S(1)}, u32[]{:S(2)}, u32[]{:S(2)}) %collective-permute-start.2) | collective-permute-done | bytes 213024 | tf_op jit(solution)/shard_map/ppermute | solution.py:261
  87.1 11.0 %all_to_all.32 = f32[4,4,16,512]{3,2,1,0:T(8,128)S(1)} all-to-all(f32[4,4,16,512]{3,2,1,0:T(8,128)S(1)} %broadcast_in_dim.11), channel_id=1, replica_groups=mesh['y'=4,'zh'=4,'core'=2,'zl'=4,'x'=4] {'y'}, dimensions={0} | all-to-all | bytes 1048576 | tf_op jit(solution)/shard_map/all_to_all | solution.py:251
  98.2 17.6 %second_sums.1 = (f32[16,16384]{1,0:T(8,128)S(1)}, f32[4,72,512]{2,1,0:T(8,128)S(1)}) custom-call(f32[24,8192]{1,0:T(8,128)S(1)} %get-tuple-element.32.values_ref.codes_ref.mine_ref.my_codes_ref, f32[24,8192]{1,0:T(8,128)S(1)} %get-tuple-element.32.values_ref.codes_ref.mine_ref.my_codes_ref, ...), custom_call_target="tpu_custom_call" | custom-call | flops 17179869184 | bytes 2097152 | tf_op jit(solution)/shard_map/second_sums/pallas_call | solution.py:211
  115.8 10.6 %all_to_all.33 = f32[4,72,512]{2,1,0:T(8,128)S(1)} all-to-all(f32[4,72,512]{2,1,0:T(8,128)S(1)} %get-tuple-element.11), channel_id=1, replica_groups=mesh['y'=4,'zh'=4,'core'=2,'zl'=4,'x'=4] {'y'}, dimensions={0} | all-to-all | bytes 1179648 | tf_op jit(solution)/shard_map/all_to_all | solution.py:265
  126.4 1.9 %collective-permute-start.3 = (f32[88,512]{1,0:T(8,128)S(1)}, f32[88,512]{1,0:T(8,128)S(1)}, u32[]{:S(2)}, u32[]{:S(2)}) collective-permute-start(f32[88,512]{1,0:T(8,128)S(1)} %pad_maximum_fusion.5), channel_id=1, source_target_pairs={{0,32},{16,112},{32,0},{48,80},{64,96},{80,48},{96,64},{112,16},{1... | collective-permute-start | bytes 540680 | tf_op jit(solution)/shard_map/ppermute | solution.py:261
  128.3 8.2 %collective-permute-done.3 = f32[88,512]{1,0:T(8,128)S(1)} collective-permute-done((f32[88,512]{1,0:T(8,128)S(1)}, f32[88,512]{1,0:T(8,128)S(1)}, u32[]{:S(2)}, u32[]{:S(2)}) %collective-permute-start.3) | collective-permute-done | bytes 180256 | tf_op jit(solution)/shard_map/ppermute | solution.py:261
  136.6 8.5 %collective-permute-start.4 = (f32[104,512]{1,0:T(8,128)S(1)}, f32[104,512]{1,0:T(8,128)S(1)}, u32[]{:S(2)}, u32[]{:S(2)}) collective-permute-start(f32[104,512]{1,0:T(8,128)S(1)} %pad_maximum_fusion.3), channel_id=1, source_target_pairs={{0,96},{16,48},{32,64},{48,16},{64,32},{80,112},{96,0},{112,80},{1... | collective-permute-start | bytes 638984 | tf_op jit(solution)/shard_map/ppermute | solution.py:261
  145.1 11.4 %collective-permute-start.5 = (f32[16,256]{1,0:T(8,128)S(1)}, f32[16,256]{1,0:T(8,128)S(1)}, u32[]{:S(2)}, u32[]{:S(2)}) collective-permute-start(f32[16,256]{1,0:T(8,128)S(1)} %get-tuple-element.40), channel_id=1, source_target_pairs={{0,16},{16,0},{1,17},{17,1},{2,18},{18,2},{3,19},{19,3},{4,20},{20... | collective-permute-start | bytes 49160 | tf_op jit(solution)/shard_map/ppermute | solution.py:255
  158.2 9.3 %all_to_all.34 = f32[4,4,16,512]{3,2,1,0:T(8,128)S(1)} all-to-all(f32[4,4,16,512]{3,2,1,0:T(8,128)S(1)} %broadcast_in_dim.12), channel_id=1, replica_groups=mesh['y'=4,'zh'=4,'core'=2,'zl'=4,'x'=4] {'y'}, dimensions={0} | all-to-all | bytes 1048576 | tf_op jit(solution)/shard_map/all_to_all | solution.py:251
  167.6 4.9 %last_lookup.2 = f32[24,8192]{1,0:T(8,128)S(1)} custom-call(f32[16,16384]{1,0:T(8,128)S(1)} %get-tuple-element.17.middle_ref, f32[24,8192]{1,0:T(8,128)S(1)} %collective-permute-done.values_ref.codes_ref.theirs_ref.their_codes_ref, f32[256,512]{1,0:T(8,128)S(1)} %bitcast.39, f32[8,8192]{1,0:T(8,128)S(1)} %broadcast_in_dim.14.refs_1_), custom_call_target="tpu_custom_call" | custom-call | flops 4294967296 | bytes 1048576 | tf_op jit(solution)/shard_map/last_lookup/pallas_call | solution.py:233
  172.5 9.4 %collective-permute-start.6 = (f32[24,8192]{1,0:T(8,128)S(1)}, f32[24,8192]{1,0:T(8,128)S(1)}, u32[]{:S(2)}, u32[]{:S(2)}) collective-permute-start(f32[24,8192]{1,0:T(8,128)S(1)} %last_lookup.2), channel_id=1, source_target_pairs={{0,16},{16,0},{1,17},{17,1},{2,18},{18,2},{3,19},{19,3},{4,20},{20... | collective-permute-start | bytes 2359304 | tf_op jit(solution)/shard_map/ppermute | solution.py:255
  181.9 4.8 %last_lookup.3 = f32[16,8192]{1,0:T(8,128)S(1)} custom-call(f32[16,16384]{1,0:T(8,128)S(1)} %get-tuple-element.17.middle_ref, f32[24,8192]{1,0:T(8,128)S(1)} %get-tuple-element.32.values_ref.codes_ref.mine_ref.my_codes_ref, f32[256,512]{1,0:T(8,128)S(1)} %bitcast.40), custom_call_target="tpu_custom_call" | custom-call | flops 4294967296 | bytes 1048576 | tf_op jit(solution)/shard_map/last_lookup/pallas_call | solution.py:233
  186.9 1.1 maximum_select_fusion
  (74 shorter events, 5.7 us)
Async XLA Ops:
  0.6 1.0 copy-start
  11.5 6.5 %copy-start.2 = (s32[8192]{0:T(1024)S(1)}, s32[8192]{0:T(1024)}, u32[]{:S(2)}) copy-start(s32[8192]{0:T(1024)} %param.7) | copy-start | bytes 98308
  11.5 6.5 %copy-start.3 = (s32[8192]{0:T(1024)S(1)}, s32[8192]{0:T(1024)}, u32[]{:S(2)}) copy-start(s32[8192]{0:T(1024)} %param.6) | copy-start | bytes 98308
  11.5 6.6 %copy-start.4 = (f32[32,256]{1,0:T(8,128)S(1)}, f32[32,256]{1,0:T(8,128)}, u32[]{:S(2)}) copy-start(f32[32,256]{1,0:T(8,128)} %param.9) | copy-start | bytes 98308
  11.5 6.6 %copy-start.5 = (f32[32,256]{1,0:T(8,128)S(1)}, f32[32,256]{1,0:T(8,128)}, u32[]{:S(2)}) copy-start(f32[32,256]{1,0:T(8,128)} %param.8) | copy-start | bytes 98308
  12.3 10.7 %copy-start.1 = (bf16[32,8192]{1,0:T(8,128)(2,1)S(1)}, bf16[32,8192]{1,0:T(8,128)(2,1)}, u32[]{:S(2)}) copy-start(bf16[32,8192]{1,0:T(8,128)(2,1)} %e_ref.1) | copy-start | bytes 1572868
  12.3 10.5 %all-to-all-start.1 = ((f32[4,1,8192]{2,1,0:T(1,128)}), f32[4,1,8192]{2,1,0:T(1,128)S(1)}, u32[]{:S(2)}, u32[]{:S(2)}) async-start(f32[4,1,8192]{2,1,0:T(1,128)} %broadcast_in_dim.10), calls=%async_computation.1 | async-start | bytes 262144 | tf_op jit(solution)/shard_map/all_to_all | solution.py:251
  23.3 10.7 %collective-permute-start = (f32[24,8192]{1,0:T(8,128)S(1)}, f32[24,8192]{1,0:T(8,128)S(1)}, u32[]{:S(2)}, u32[]{:S(2)}) collective-permute-start(f32[24,8192]{1,0:T(8,128)S(1)} %get-tuple-element.31), channel_id=1, source_target_pairs={{0,16},{16,0},{1,17},{17,1},{2,18},{18,2},{3,19},{19,3},{4,20},{20... | collective-permute-start | bytes 2359304 | tf_op jit(solution)/shard_map/ppermute | solution.py:255
  39.1 13.8 %all-to-all-start.2 = ((f32[4,72,512]{2,1,0:T(8,128)}), f32[4,72,512]{2,1,0:T(8,128)S(1)}, u32[]{:S(2)}, u32[]{:S(2)}) async-start(f32[4,72,512]{2,1,0:T(8,128)} %first_sums.3), calls=%async_computation.2 | async-start | bytes 1179648 | tf_op jit(solution)/shard_map/all_to_all | solution.py:265
  53.0 17.4 %collective-permute-start.1 = (f32[88,512]{1,0:T(8,128)S(1)}, f32[88,512]{1,0:T(8,128)S(1)}, u32[]{:S(2)}, u32[]{:S(2)}) collective-permute-start(f32[88,512]{1,0:T(8,128)S(1)} %pad_maximum_fusion.4), channel_id=1, source_target_pairs={{0,32},{16,112},{32,0},{48,80},{64,96},{80,48},{96,64},{112,16},{1... | collective-permute-start | bytes 540680 | tf_op jit(solution)/shard_map/ppermute | solution.py:261
  70.4 16.5 %collective-permute-start.2 = (f32[104,512]{1,0:T(8,128)S(1)}, f32[104,512]{1,0:T(8,128)S(1)}, u32[]{:S(2)}, u32[]{:S(2)}) collective-permute-start(f32[104,512]{1,0:T(8,128)S(1)} %pad_maximum_fusion.2), channel_id=1, source_target_pairs={{0,96},{16,48},{32,64},{48,16},{64,32},{80,112},{96,0},{112,80},{1... | collective-permute-start | bytes 638984 | tf_op jit(solution)/shard_map/ppermute | solution.py:261
  126.4 10.1 %collective-permute-start.3 = (f32[88,512]{1,0:T(8,128)S(1)}, f32[88,512]{1,0:T(8,128)S(1)}, u32[]{:S(2)}, u32[]{:S(2)}) collective-permute-start(f32[88,512]{1,0:T(8,128)S(1)} %pad_maximum_fusion.5), channel_id=1, source_target_pairs={{0,32},{16,112},{32,0},{48,80},{64,96},{80,48},{96,64},{112,16},{1... | collective-permute-start | bytes 540680 | tf_op jit(solution)/shard_map/ppermute | solution.py:261
  136.6 21.4 %collective-permute-start.4 = (f32[104,512]{1,0:T(8,128)S(1)}, f32[104,512]{1,0:T(8,128)S(1)}, u32[]{:S(2)}, u32[]{:S(2)}) collective-permute-start(f32[104,512]{1,0:T(8,128)S(1)} %pad_maximum_fusion.3), channel_id=1, source_target_pairs={{0,96},{16,48},{32,64},{48,16},{64,32},{80,112},{96,0},{112,80},{1... | collective-permute-start | bytes 638984 | tf_op jit(solution)/shard_map/ppermute | solution.py:261
  145.1 12.3 %collective-permute-start.5 = (f32[16,256]{1,0:T(8,128)S(1)}, f32[16,256]{1,0:T(8,128)S(1)}, u32[]{:S(2)}, u32[]{:S(2)}) collective-permute-start(f32[16,256]{1,0:T(8,128)S(1)} %get-tuple-element.40), channel_id=1, source_target_pairs={{0,16},{16,0},{1,17},{17,1},{2,18},{18,2},{3,19},{19,3},{4,20},{20... | collective-permute-start | bytes 49160 | tf_op jit(solution)/shard_map/ppermute | solution.py:255
  172.5 14.3 %collective-permute-start.6 = (f32[24,8192]{1,0:T(8,128)S(1)}, f32[24,8192]{1,0:T(8,128)S(1)}, u32[]{:S(2)}, u32[]{:S(2)}) collective-permute-start(f32[24,8192]{1,0:T(8,128)S(1)} %last_lookup.2), channel_id=1, source_target_pairs={{0,16},{16,0},{1,17},{17,1},{2,18},{18,2},{3,19},{19,3},{4,20},{20... | collective-permute-start | bytes 2359304 | tf_op jit(solution)/shard_map/ppermute | solution.py:255

commit v4 on v3

--- a/solution.py
+++ b/solution.py
@@ -255,8 +255,8 @@
     return lax.ppermute(v, "core", [(0, 1), (1, 0)])
 
 
-def swap_z(v, first):
-    steps = (1, 3) if first else (3, 1)
+def swap_z(v, step):
+    steps = ((1, 3), (3, 1))[step]
     pairs = [(2 * z + c, 2 * (z ^ steps[c]) + c) for z in range(Z) for c in range(2)]
     return lax.ppermute(v, ("zh", "core"), pairs)
 
@@ -265,17 +265,14 @@
     return [lax.all_to_all(part, "y", 0, 0, tiled=True).sum(axis=0) for part in parts]
 
 
-def over_z(parts, first):
-    return [part + swap_z(part, first) for part in parts]
-
-
-def over_z_with(parts, old, core, zh):
+def over_z_with(parts, old, core, zh, order):
     (own,) = parts
-    got = swap_z(jnp.concatenate([own, old]), True)
+    got = swap_z(jnp.concatenate([own, old]), order[0])
     own, olds = own + got[:BLOCK], [old, got[BLOCK:]]
-    got = swap_z(jnp.concatenate([own, *olds]), False)
-    own, olds = own + got[:BLOCK], jnp.stack([*olds, got[BLOCK : BLOCK + F], got[BLOCK + F :]])
-    near, far = jnp.where(core == 0, olds[1], olds[2]), jnp.where(core == 0, olds[2], olds[1])
+    got = swap_z(jnp.concatenate([own, *olds]), order[1])
+    own, olds = own + got[:BLOCK], [*olds, got[BLOCK : BLOCK + F], got[BLOCK + F :]]
+    near_first = core == order[0]
+    near, far = jnp.where(near_first, olds[1], olds[2]), jnp.where(near_first, olds[2], olds[1])
     olds = jnp.stack([olds[0], near, olds[3], far])
     olds = jnp.where(zh % 2 == 0, olds, jnp.stack([olds[1], olds[0], olds[3], olds[2]]))
     olds = jnp.where(zh < 2, olds, jnp.concatenate([olds[2:], olds[:2]]))
@@ -325,12 +322,12 @@
 
     sums = first_sums(theirs, first_sums(mine))
     olds = by_core(mine[F + 2].reshape(2, F, 256), theirs[F + 2].reshape(2, F, 256), 2)
-    own, old = over_z_with(at_y(sums), olds[0], core, zh)
+    own, old = over_z_with(at_y(sums), olds[0], core, zh, (0, 1))
     first_news = updated(own, old)
 
     middle, *sums = second_sums(mine, theirs, tables_of(first_news))
     own, first_news = lax.optimization_barrier((at_y(sums), first_news))
-    own, old = over_z_with(own, olds[1], core, zh)
+    own, old = over_z_with(own, olds[1], core, zh, (1, 0))
     kept, sent = owned(first_news)
     own, first_new = lax.optimization_barrier((own, by_core(kept, swap_core(sent), 0)))
     second_news = updated(own, old)

time: 189 us -> 187 us (0.989)
  the two profiles are of different devices: /device:TPU:1 before, /device:TPU:33 now
where the time goes in v4:
time: 187 us; the launch traced here: 186 us
  starting transfers between devices  71.2 us (38%)
  blocking collectives  37 us (20%)
  Pallas kernels  36.8 us (20%)
  waiting for transfers between devices  34.1 us (18%)
  other arithmetic  3.29 us (2%)
  local copies, waits for them, and re-layouts  2.43 us (1%)
    ppermute x4, starting transfers between devices, swap_z(): return lax.ppermute(v, ('zh', 'core'), pairs)  35.6 us
    ppermute x3, starting transfers between devices, swap_core(): return lax.ppermute(v, 'core', [(0, 1), (1, 0)])  26.5 us
    ppermute x4, waiting for transfers between devices, swap_z(): return lax.ppermute(v, ('zh', 'core'), pairs)  19.1 us
    all_to_all x2, blocking collectives, to_all(): lax.all_to_all(jnp.broadcast_to(v[None], (size, *v.shape)), axis, 0, 0, t...  18.7 us
    pallas_call x1, Pallas kernels, second_sums(): pl.pallas_call(functools.partial(second_kernel, tiles), grid=(2 * tiles,)...  17.6 us
    all_to_all x1, waiting for transfers between devices, at_y(): lax.all_to_all(part, 'y', 0, 0, tiled=True).sum(axis=0)  10.2 us
    pallas_call x2, Pallas kernels, last_lookup(): pl.pallas_call(last_kernel, grid=(tiles,), in_specs=[pl.BlockSpec((F, TIL...  9.71 us
    all_to_all x1, blocking collectives, at_y(): lax.all_to_all(part, 'y', 0, 0, tiled=True).sum(axis=0)  9.67 us
  transfers between devices with their start and end apart: 9, of which 6 were waited for; matrix products, arithmetic and copies ran while one was open for 1% of the time, Pallas kernels for 5%

profile of v4, /device:TPU:33, one launch (start us, length us, event | category | flops | bytes accessed | tf_op | source)
XLA Modules:
  0.0 185.9 jit_solution(11331226843506367188)
XLA Ops:
  1.9 8.6 %all_to_all.31 = f32[4,1,8192]{2,1,0:T(1,128)S(1)} all-to-all(f32[4,1,8192]{2,1,0:T(1,128)S(1)} %squares.1), channel_id=1, replica_groups=mesh['y'=4,'zh'=4,'core'=2,'zl'=4,'x'=4] {'x'}, dimensions={0} | all-to-all | bytes 262144 | tf_op jit(solution)/shard_map/all_to_all | solution.py:311
  11.4 5.6 %all-to-all-start.1 = ((f32[4,1,8192]{2,1,0:T(1,128)}), f32[4,1,8192]{2,1,0:T(1,128)S(1)}, u32[]{:S(2)}, u32[]{:S(2)}) async-start(f32[4,1,8192]{2,1,0:T(1,128)} %broadcast_in_dim.10), calls=%async_computation.1 | async-start | bytes 262144 | tf_op jit(solution)/shard_map/all_to_all | solution.py:251
  17.3 4.0 %all-to-all-done.1 = f32[4,1,8192]{2,1,0:T(1,128)S(1)} async-done(((f32[4,1,8192]{2,1,0:T(1,128)}), f32[4,1,8192]{2,1,0:T(1,128)S(1)}, u32[]{:S(2)}, u32[]{:S(2)}) %all-to-all-start.1) | async-done | bytes 131104 | tf_op jit(solution)/shard_map/all_to_all | solution.py:251
  21.8 6.5 %collective-permute-start = (f32[24,8192]{1,0:T(8,128)S(1)}, f32[24,8192]{1,0:T(8,128)S(1)}, u32[]{:S(2)}, u32[]{:S(2)}) collective-permute-start(f32[24,8192]{1,0:T(8,128)S(1)} %get-tuple-element.31), channel_id=1, source_target_pairs={{0,16},{16,0},{1,17},{17,1},{2,18},{18,2},{3,19},{19,3},{4,20},{20... | collective-permute-start | bytes 2359304 | tf_op jit(solution)/shard_map/ppermute | solution.py:255
  28.4 4.2 %first_sums.2.refs_0_ = f32[4,72,512]{2,1,0:T(8,128)S(1)} custom-call(f32[24,8192]{1,0:T(8,128)S(1)} %get-tuple-element.32.values_ref.codes_ref.mine_ref.my_codes_ref, f32[24,8192]{1,0:T(8,128)S(1)} %get-tuple-element.32.values_ref.codes_ref.mine_ref.my_codes_ref), custom_call_target="tpu_custom_call" | custom-call | flops 4294967296 | bytes 1048576 | tf_op jit(solution)/shard_map/first_sums/pallas_call | solution.py:188
  32.6 5.0 %first_sums.3 = f32[4,72,512]{2,1,0:T(8,128)} custom-call(f32[24,8192]{1,0:T(8,128)S(1)} %collective-permute-done.values_ref.codes_ref.theirs_ref.their_codes_ref, f32[24,8192]{1,0:T(8,128)S(1)} %collective-permute-done.values_ref.codes_ref.theirs_ref.their_codes_ref, f32[4,72,512]{2,1,0:T(8,128)S(1)} %first_sums.2.refs_0_), custom_call_target="tpu_custom_call" | custom-call | flops 4294967296 | bytes 1048576 | tf_op jit(solution)/shard_map/first_sums/pallas_call | solution.py:188
  37.6 3.5 %all-to-all-start.2 = ((f32[4,72,512]{2,1,0:T(8,128)}), f32[4,72,512]{2,1,0:T(8,128)S(1)}, u32[]{:S(2)}, u32[]{:S(2)}) async-start(f32[4,72,512]{2,1,0:T(8,128)} %first_sums.3), calls=%async_computation.2 | async-start | bytes 1179648 | tf_op jit(solution)/shard_map/all_to_all | solution.py:265
  41.2 10.2 %all-to-all-done.2 = f32[4,72,512]{2,1,0:T(8,128)S(1)} async-done(((f32[4,72,512]{2,1,0:T(8,128)}), f32[4,72,512]{2,1,0:T(8,128)S(1)}, u32[]{:S(2)}, u32[]{:S(2)}) %all-to-all-start.2) | async-done | bytes 589856 | tf_op jit(solution)/shard_map/all_to_all | solution.py:265
  51.5 9.2 %collective-permute-start.1 = (f32[88,512]{1,0:T(8,128)S(1)}, f32[88,512]{1,0:T(8,128)S(1)}, u32[]{:S(2)}, u32[]{:S(2)}) collective-permute-start(f32[88,512]{1,0:T(8,128)S(1)} %pad_maximum_fusion.4), channel_id=1, source_target_pairs={{0,32},{16,112},{32,0},{48,80},{64,96},{80,48},{96,64},{112,16},{1... | collective-permute-start | bytes 540680 | tf_op jit(solution)/shard_map/ppermute | solution.py:261
  60.7 6.4 %collective-permute-done.1 = f32[88,512]{1,0:T(8,128)S(1)} collective-permute-done((f32[88,512]{1,0:T(8,128)S(1)}, f32[88,512]{1,0:T(8,128)S(1)}, u32[]{:S(2)}, u32[]{:S(2)}) %collective-permute-start.1) | collective-permute-done | bytes 180256 | tf_op jit(solution)/shard_map/ppermute | solution.py:261
  67.1 7.1 %collective-permute-start.2 = (f32[104,512]{1,0:T(8,128)S(1)}, f32[104,512]{1,0:T(8,128)S(1)}, u32[]{:S(2)}, u32[]{:S(2)}) collective-permute-start(f32[104,512]{1,0:T(8,128)S(1)} %pad_maximum_fusion.2), channel_id=1, source_target_pairs={{0,96},{16,48},{32,64},{48,16},{64,32},{80,112},{96,0},{112,80},{1... | collective-permute-start | bytes 638984 | tf_op jit(solution)/shard_map/ppermute | solution.py:261
  74.2 9.3 %collective-permute-done.2 = f32[104,512]{1,0:T(8,128)S(1)} collective-permute-done((f32[104,512]{1,0:T(8,128)S(1)}, f32[104,512]{1,0:T(8,128)S(1)}, u32[]{:S(2)}, u32[]{:S(2)}) %collective-permute-start.2) | collective-permute-done | bytes 213024 | tf_op jit(solution)/shard_map/ppermute | solution.py:261
  83.7 9.3 %all_to_all.32 = f32[4,4,16,512]{3,2,1,0:T(8,128)S(1)} all-to-all(f32[4,4,16,512]{3,2,1,0:T(8,128)S(1)} %broadcast_in_dim.11), channel_id=1, replica_groups=mesh['y'=4,'zh'=4,'core'=2,'zl'=4,'x'=4] {'y'}, dimensions={0} | all-to-all | bytes 1048576 | tf_op jit(solution)/shard_map/all_to_all | solution.py:251
  93.0 17.6 %second_sums.1 = (f32[16,16384]{1,0:T(8,128)S(1)}, f32[4,72,512]{2,1,0:T(8,128)S(1)}) custom-call(f32[24,8192]{1,0:T(8,128)S(1)} %get-tuple-element.32.values_ref.codes_ref.mine_ref.my_codes_ref, f32[24,8192]{1,0:T(8,128)S(1)} %get-tuple-element.32.values_ref.codes_ref.mine_ref.my_codes_ref, ...), custom_call_target="tpu_custom_call" | custom-call | flops 17179869184 | bytes 2097152 | tf_op jit(solution)/shard_map/second_sums/pallas_call | solution.py:211
  110.6 9.7 %all_to_all.33 = f32[4,72,512]{2,1,0:T(8,128)S(1)} all-to-all(f32[4,72,512]{2,1,0:T(8,128)S(1)} %get-tuple-element.11), channel_id=1, replica_groups=mesh['y'=4,'zh'=4,'core'=2,'zl'=4,'x'=4] {'y'}, dimensions={0} | all-to-all | bytes 1179648 | tf_op jit(solution)/shard_map/all_to_all | solution.py:265
  120.3 11.4 %collective-permute-start.3 = (f32[88,512]{1,0:T(8,128)S(1)}, f32[88,512]{1,0:T(8,128)S(1)}, u32[]{:S(2)}, u32[]{:S(2)}) collective-permute-start(f32[88,512]{1,0:T(8,128)S(1)} %pad_maximum_fusion.5), channel_id=1, source_target_pairs={{0,96},{16,48},{32,64},{48,16},{64,32},{80,112},{96,0},{112,80},{1... | collective-permute-start | bytes 540680 | tf_op jit(solution)/shard_map/ppermute | solution.py:261
  131.8 3.5 %collective-permute-done.3 = f32[88,512]{1,0:T(8,128)S(1)} collective-permute-done((f32[88,512]{1,0:T(8,128)S(1)}, f32[88,512]{1,0:T(8,128)S(1)}, u32[]{:S(2)}, u32[]{:S(2)}) %collective-permute-start.3) | collective-permute-done | bytes 180256 | tf_op jit(solution)/shard_map/ppermute | solution.py:261
  135.3 8.0 %collective-permute-start.4 = (f32[104,512]{1,0:T(8,128)S(1)}, f32[104,512]{1,0:T(8,128)S(1)}, u32[]{:S(2)}, u32[]{:S(2)}) collective-permute-start(f32[104,512]{1,0:T(8,128)S(1)} %pad_maximum_fusion.3), channel_id=1, source_target_pairs={{0,32},{16,112},{32,0},{48,80},{64,96},{80,48},{96,64},{112,16},{1... | collective-permute-start | bytes 638984 | tf_op jit(solution)/shard_map/ppermute | solution.py:261
  143.3 11.8 %collective-permute-start.5 = (f32[16,256]{1,0:T(8,128)S(1)}, f32[16,256]{1,0:T(8,128)S(1)}, u32[]{:S(2)}, u32[]{:S(2)}) collective-permute-start(f32[16,256]{1,0:T(8,128)S(1)} %get-tuple-element.40), channel_id=1, source_target_pairs={{0,16},{16,0},{1,17},{17,1},{2,18},{18,2},{3,19},{19,3},{4,20},{20... | collective-permute-start | bytes 49160 | tf_op jit(solution)/shard_map/ppermute | solution.py:255
  156.7 9.3 %all_to_all.34 = f32[4,4,16,512]{3,2,1,0:T(8,128)S(1)} all-to-all(f32[4,4,16,512]{3,2,1,0:T(8,128)S(1)} %broadcast_in_dim.12), channel_id=1, replica_groups=mesh['y'=4,'zh'=4,'core'=2,'zl'=4,'x'=4] {'y'}, dimensions={0} | all-to-all | bytes 1048576 | tf_op jit(solution)/shard_map/all_to_all | solution.py:251
  166.1 4.9 %last_lookup.2 = f32[24,8192]{1,0:T(8,128)S(1)} custom-call(f32[16,16384]{1,0:T(8,128)S(1)} %get-tuple-element.17.middle_ref, f32[24,8192]{1,0:T(8,128)S(1)} %collective-permute-done.values_ref.codes_ref.theirs_ref.their_codes_ref, f32[256,512]{1,0:T(8,128)S(1)} %bitcast.39, f32[8,8192]{1,0:T(8,128)S(1)} %broadcast_in_dim.14.refs_1_), custom_call_target="tpu_custom_call" | custom-call | flops 4294967296 | bytes 1048576 | tf_op jit(solution)/shard_map/last_lookup/pallas_call | solution.py:233
  171.0 8.3 %collective-permute-start.6 = (f32[24,8192]{1,0:T(8,128)S(1)}, f32[24,8192]{1,0:T(8,128)S(1)}, u32[]{:S(2)}, u32[]{:S(2)}) collective-permute-start(f32[24,8192]{1,0:T(8,128)S(1)} %last_lookup.2), channel_id=1, source_target_pairs={{0,16},{16,0},{1,17},{17,1},{2,18},{18,2},{3,19},{19,3},{4,20},{20... | collective-permute-start | bytes 2359304 | tf_op jit(solution)/shard_map/ppermute | solution.py:255
  179.3 4.8 %last_lookup.3 = f32[16,8192]{1,0:T(8,128)S(1)} custom-call(f32[16,16384]{1,0:T(8,128)S(1)} %get-tuple-element.17.middle_ref, f32[24,8192]{1,0:T(8,128)S(1)} %get-tuple-element.32.values_ref.codes_ref.mine_ref.my_codes_ref, f32[256,512]{1,0:T(8,128)S(1)} %bitcast.40), custom_call_target="tpu_custom_call" | custom-call | flops 4294967296 | bytes 1048576 | tf_op jit(solution)/shard_map/last_lookup/pallas_call | solution.py:233
  184.2 1.1 maximum_select_fusion
  (74 shorter events, 5.7 us)
Async XLA Ops:
  0.6 1.0 copy-start
  10.7 6.3 %copy-start.2 = (s32[8192]{0:T(1024)S(1)}, s32[8192]{0:T(1024)}, u32[]{:S(2)}) copy-start(s32[8192]{0:T(1024)} %param.7) | copy-start | bytes 98308
  10.7 6.3 %copy-start.3 = (s32[8192]{0:T(1024)S(1)}, s32[8192]{0:T(1024)}, u32[]{:S(2)}) copy-start(s32[8192]{0:T(1024)} %param.6) | copy-start | bytes 98308
  10.7 6.4 %copy-start.4 = (f32[32,256]{1,0:T(8,128)S(1)}, f32[32,256]{1,0:T(8,128)}, u32[]{:S(2)}) copy-start(f32[32,256]{1,0:T(8,128)} %param.9) | copy-start | bytes 98308
  10.7 6.4 %copy-start.5 = (f32[32,256]{1,0:T(8,128)S(1)}, f32[32,256]{1,0:T(8,128)}, u32[]{:S(2)}) copy-start(f32[32,256]{1,0:T(8,128)} %param.8) | copy-start | bytes 98308
  11.4 10.0 %copy-start.1 = (bf16[32,8192]{1,0:T(8,128)(2,1)S(1)}, bf16[32,8192]{1,0:T(8,128)(2,1)}, u32[]{:S(2)}) copy-start(bf16[32,8192]{1,0:T(8,128)(2,1)} %e_ref.1) | copy-start | bytes 1572868
  11.4 9.9 %all-to-all-start.1 = ((f32[4,1,8192]{2,1,0:T(1,128)}), f32[4,1,8192]{2,1,0:T(1,128)S(1)}, u32[]{:S(2)}, u32[]{:S(2)}) async-start(f32[4,1,8192]{2,1,0:T(1,128)} %broadcast_in_dim.10), calls=%async_computation.1 | async-start | bytes 262144 | tf_op jit(solution)/shard_map/all_to_all | solution.py:251
  21.8 10.7 %collective-permute-start = (f32[24,8192]{1,0:T(8,128)S(1)}, f32[24,8192]{1,0:T(8,128)S(1)}, u32[]{:S(2)}, u32[]{:S(2)}) collective-permute-start(f32[24,8192]{1,0:T(8,128)S(1)} %get-tuple-element.31), channel_id=1, source_target_pairs={{0,16},{16,0},{1,17},{17,1},{2,18},{18,2},{3,19},{19,3},{4,20},{20... | collective-permute-start | bytes 2359304 | tf_op jit(solution)/shard_map/ppermute | solution.py:255
  37.6 13.8 %all-to-all-start.2 = ((f32[4,72,512]{2,1,0:T(8,128)}), f32[4,72,512]{2,1,0:T(8,128)S(1)}, u32[]{:S(2)}, u32[]{:S(2)}) async-start(f32[4,72,512]{2,1,0:T(8,128)} %first_sums.3), calls=%async_computation.2 | async-start | bytes 1179648 | tf_op jit(solution)/shard_map/all_to_all | solution.py:265
  51.5 15.6 %collective-permute-start.1 = (f32[88,512]{1,0:T(8,128)S(1)}, f32[88,512]{1,0:T(8,128)S(1)}, u32[]{:S(2)}, u32[]{:S(2)}) collective-permute-start(f32[88,512]{1,0:T(8,128)S(1)} %pad_maximum_fusion.4), channel_id=1, source_target_pairs={{0,32},{16,112},{32,0},{48,80},{64,96},{80,48},{96,64},{112,16},{1... | collective-permute-start | bytes 540680 | tf_op jit(solution)/shard_map/ppermute | solution.py:261
  67.1 16.3 %collective-permute-start.2 = (f32[104,512]{1,0:T(8,128)S(1)}, f32[104,512]{1,0:T(8,128)S(1)}, u32[]{:S(2)}, u32[]{:S(2)}) collective-permute-start(f32[104,512]{1,0:T(8,128)S(1)} %pad_maximum_fusion.2), channel_id=1, source_target_pairs={{0,96},{16,48},{32,64},{48,16},{64,32},{80,112},{96,0},{112,80},{1... | collective-permute-start | bytes 638984 | tf_op jit(solution)/shard_map/ppermute | solution.py:261
  120.3 14.9 %collective-permute-start.3 = (f32[88,512]{1,0:T(8,128)S(1)}, f32[88,512]{1,0:T(8,128)S(1)}, u32[]{:S(2)}, u32[]{:S(2)}) collective-permute-start(f32[88,512]{1,0:T(8,128)S(1)} %pad_maximum_fusion.5), channel_id=1, source_target_pairs={{0,96},{16,48},{32,64},{48,16},{64,32},{80,112},{96,0},{112,80},{1... | collective-permute-start | bytes 540680 | tf_op jit(solution)/shard_map/ppermute | solution.py:261
  135.3 21.2 %collective-permute-start.4 = (f32[104,512]{1,0:T(8,128)S(1)}, f32[104,512]{1,0:T(8,128)S(1)}, u32[]{:S(2)}, u32[]{:S(2)}) collective-permute-start(f32[104,512]{1,0:T(8,128)S(1)} %pad_maximum_fusion.3), channel_id=1, source_target_pairs={{0,32},{16,112},{32,0},{48,80},{64,96},{80,48},{96,64},{112,16},{1... | collective-permute-start | bytes 638984 | tf_op jit(solution)/shard_map/ppermute | solution.py:261
  143.3 12.6 %collective-permute-start.5 = (f32[16,256]{1,0:T(8,128)S(1)}, f32[16,256]{1,0:T(8,128)S(1)}, u32[]{:S(2)}, u32[]{:S(2)}) collective-permute-start(f32[16,256]{1,0:T(8,128)S(1)} %get-tuple-element.40), channel_id=1, source_target_pairs={{0,16},{16,0},{1,17},{17,1},{2,18},{18,2},{3,19},{19,3},{4,20},{20... | collective-permute-start | bytes 49160 | tf_op jit(solution)/shard_map/ppermute | solution.py:255
  171.0 13.1 %collective-permute-start.6 = (f32[24,8192]{1,0:T(8,128)S(1)}, f32[24,8192]{1,0:T(8,128)S(1)}, u32[]{:S(2)}, u32[]{:S(2)}) collective-permute-start(f32[24,8192]{1,0:T(8,128)S(1)} %last_lookup.2), channel_id=1, source_target_pairs={{0,16},{16,0},{1,17},{17,1},{2,18},{18,2},{3,19},{19,3},{4,20},{20... | collective-permute-start | bytes 2359304 | tf_op jit(solution)/shard_map/ppermute | solution.py:255

commit v5 on v4

--- a/solution.py
+++ b/solution.py
@@ -265,9 +265,10 @@
     return [lax.all_to_all(part, "y", 0, 0, tiled=True).sum(axis=0) for part in parts]
 
 
-def over_z_with(parts, old, core, zh, order):
+def over_z_with(parts, old, core, zh, order, beside=()):
     (own,) = parts
     got = swap_z(jnp.concatenate([own, old]), order[0])
+    got, beside = lax.optimization_barrier((got, beside))
     own, olds = own + got[:BLOCK], [old, got[BLOCK:]]
     got = swap_z(jnp.concatenate([own, *olds]), order[1])
     own, olds = own + got[:BLOCK], [*olds, got[BLOCK : BLOCK + F], got[BLOCK + F :]]
@@ -276,7 +277,7 @@
     olds = jnp.stack([olds[0], near, olds[3], far])
     olds = jnp.where(zh % 2 == 0, olds, jnp.stack([olds[1], olds[0], olds[3], olds[2]]))
     olds = jnp.where(zh < 2, olds, jnp.concatenate([olds[2:], olds[:2]]))
-    return [own], olds
+    return [own], olds, beside
 
 
 def updated(parts, olds):
@@ -322,14 +323,14 @@
 
     sums = first_sums(theirs, first_sums(mine))
     olds = by_core(mine[F + 2].reshape(2, F, 256), theirs[F + 2].reshape(2, F, 256), 2)
-    own, old = over_z_with(at_y(sums), olds[0], core, zh, (0, 1))
+    own, old, _ = over_z_with(at_y(sums), olds[0], core, zh, (0, 1))
     first_news = updated(own, old)
 
     middle, *sums = second_sums(mine, theirs, tables_of(first_news))
     own, first_news = lax.optimization_barrier((at_y(sums), first_news))
-    own, old = over_z_with(own, olds[1], core, zh, (1, 0))
     kept, sent = owned(first_news)
-    own, first_new = lax.optimization_barrier((own, by_core(kept, swap_core(sent), 0)))
+    first_new = by_core(kept, swap_core(sent), 0)
+    own, old, first_new = over_z_with(own, olds[1], core, zh, (1, 0), first_new)
     second_news = updated(own, old)
 
     tables, second_news = lax.optimization_barrier((tables_of(second_news), second_news))

time: 187 us -> 187 us (level)
  the two profiles are of different devices: /device:TPU:33 before, /device:TPU:1 now
where the time goes in v5:
time: 187 us; the launch traced here: 186 us
  starting transfers between devices  60.1 us (32%)
  waiting for transfers between devices  50.9 us (27%)
  Pallas kernels  37.5 us (20%)
  blocking collectives  30.4 us (16%)
  other arithmetic  3.29 us (2%)
  local copies, waits for them, and re-layouts  2.43 us (1%)
    ppermute x4, waiting for transfers between devices, swap_z(): return lax.ppermute(v, ('zh', 'core'), pairs)  26.8 us
    ppermute x3, starting transfers between devices, swap_core(): return lax.ppermute(v, 'core', [(0, 1), (1, 0)])  24.6 us
    ppermute x4, starting transfers between devices, swap_z(): return lax.ppermute(v, ('zh', 'core'), pairs)  22.8 us
    all_to_all x2, blocking collectives, to_all(): lax.all_to_all(jnp.broadcast_to(v[None], (size, *v.shape)), axis, 0, 0, t...  21 us
    all_to_all x2, waiting for transfers between devices, at_y(): lax.all_to_all(part, 'y', 0, 0, tiled=True).sum(axis=0)  18.8 us
    pallas_call x1, Pallas kernels, second_sums(): pl.pallas_call(functools.partial(second_kernel, tiles), grid=(2 * tiles,)...  18.4 us
    pallas_call x2, Pallas kernels, last_lookup(): pl.pallas_call(last_kernel, grid=(tiles,), in_specs=[pl.BlockSpec((F, TIL...  9.7 us
    all_to_all x1, blocking collectives, on_device(): lax.all_to_all(squares_of(e, 4), 'x', 0, 0, tiled=True).reshape(4, n)  9.47 us
  transfers between devices with their start and end apart: 10, of which 8 were waited for; matrix products, arithmetic and copies ran while one was open for 1% of the time, Pallas kernels for 5%

profile of v5, /device:TPU:1, one launch (start us, length us, event | category | flops | bytes accessed | tf_op | source)
XLA Modules:
  0.0 185.9 jit_solution(6520923952989424446)
XLA Ops:
  1.9 9.5 %all_to_all.31 = f32[4,1,8192]{2,1,0:T(1,128)S(1)} all-to-all(f32[4,1,8192]{2,1,0:T(1,128)S(1)} %squares.1), channel_id=1, replica_groups=mesh['y'=4,'zh'=4,'core'=2,'zl'=4,'x'=4] {'x'}, dimensions={0} | all-to-all | bytes 262144 | tf_op jit(solution)/shard_map/all_to_all | solution.py:312
  12.3 5.7 %all-to-all-start.1 = ((f32[4,1,8192]{2,1,0:T(1,128)}), f32[4,1,8192]{2,1,0:T(1,128)S(1)}, u32[]{:S(2)}, u32[]{:S(2)}) async-start(f32[4,1,8192]{2,1,0:T(1,128)} %broadcast_in_dim.10), calls=%async_computation.1 | async-start | bytes 262144 | tf_op jit(solution)/shard_map/all_to_all | solution.py:251
  18.3 4.5 %all-to-all-done.1 = f32[4,1,8192]{2,1,0:T(1,128)S(1)} async-done(((f32[4,1,8192]{2,1,0:T(1,128)}), f32[4,1,8192]{2,1,0:T(1,128)S(1)}, u32[]{:S(2)}, u32[]{:S(2)}) %all-to-all-start.1) | async-done | bytes 131104 | tf_op jit(solution)/shard_map/all_to_all | solution.py:251
  23.3 6.5 %collective-permute-start = (f32[24,8192]{1,0:T(8,128)S(1)}, f32[24,8192]{1,0:T(8,128)S(1)}, u32[]{:S(2)}, u32[]{:S(2)}) collective-permute-start(f32[24,8192]{1,0:T(8,128)S(1)} %get-tuple-element.32), channel_id=1, source_target_pairs={{0,16},{16,0},{1,17},{17,1},{2,18},{18,2},{3,19},{19,3},{4,20},{20... | collective-permute-start | bytes 2359304 | tf_op jit(solution)/shard_map/ppermute | solution.py:255
  29.8 4.2 %first_sums.2.refs_0_ = f32[4,72,512]{2,1,0:T(8,128)S(1)} custom-call(f32[24,8192]{1,0:T(8,128)S(1)} %get-tuple-element.31.values_ref.codes_ref.mine_ref.my_codes_ref, f32[24,8192]{1,0:T(8,128)S(1)} %get-tuple-element.31.values_ref.codes_ref.mine_ref.my_codes_ref), custom_call_target="tpu_custom_call" | custom-call | flops 4294967296 | bytes 1048576 | tf_op jit(solution)/shard_map/first_sums/pallas_call | solution.py:188
  34.1 5.0 %first_sums.3 = f32[4,72,512]{2,1,0:T(8,128)} custom-call(f32[24,8192]{1,0:T(8,128)S(1)} %collective-permute-done.values_ref.codes_ref.theirs_ref.their_codes_ref, f32[24,8192]{1,0:T(8,128)S(1)} %collective-permute-done.values_ref.codes_ref.theirs_ref.their_codes_ref, f32[4,72,512]{2,1,0:T(8,128)S(1)} %first_sums.2.refs_0_), custom_call_target="tpu_custom_call" | custom-call | flops 4294967296 | bytes 1048576 | tf_op jit(solution)/shard_map/first_sums/pallas_call | solution.py:188
  39.1 3.5 %all-to-all-start.2 = ((f32[4,72,512]{2,1,0:T(8,128)}), f32[4,72,512]{2,1,0:T(8,128)S(1)}, u32[]{:S(2)}, u32[]{:S(2)}) async-start(f32[4,72,512]{2,1,0:T(8,128)} %first_sums.3), calls=%async_computation.2 | async-start | bytes 1179648 | tf_op jit(solution)/shard_map/all_to_all | solution.py:265
  42.7 10.2 %all-to-all-done.2 = f32[4,72,512]{2,1,0:T(8,128)S(1)} async-done(((f32[4,72,512]{2,1,0:T(8,128)}), f32[4,72,512]{2,1,0:T(8,128)S(1)}, u32[]{:S(2)}, u32[]{:S(2)}) %all-to-all-start.2) | async-done | bytes 589856 | tf_op jit(solution)/shard_map/all_to_all | solution.py:265
  52.9 9.2 %collective-permute-start.1 = (f32[88,512]{1,0:T(8,128)S(1)}, f32[88,512]{1,0:T(8,128)S(1)}, u32[]{:S(2)}, u32[]{:S(2)}) collective-permute-start(f32[88,512]{1,0:T(8,128)S(1)} %pad_maximum_fusion.4), channel_id=1, source_target_pairs={{0,32},{16,112},{32,0},{48,80},{64,96},{80,48},{96,64},{112,16},{1... | collective-permute-start | bytes 540680 | tf_op jit(solution)/shard_map/ppermute | solution.py:261
  62.1 8.2 %collective-permute-done.1 = f32[88,512]{1,0:T(8,128)S(1)} collective-permute-done((f32[88,512]{1,0:T(8,128)S(1)}, f32[88,512]{1,0:T(8,128)S(1)}, u32[]{:S(2)}, u32[]{:S(2)}) %collective-permute-start.1) | collective-permute-done | bytes 180256 | tf_op jit(solution)/shard_map/ppermute | solution.py:261
  70.4 6.7 %collective-permute-start.2 = (f32[104,512]{1,0:T(8,128)S(1)}, f32[104,512]{1,0:T(8,128)S(1)}, u32[]{:S(2)}, u32[]{:S(2)}) collective-permute-start(f32[104,512]{1,0:T(8,128)S(1)} %pad_maximum_fusion.2), channel_id=1, source_target_pairs={{0,96},{16,48},{32,64},{48,16},{64,32},{80,112},{96,0},{112,80},{1... | collective-permute-start | bytes 638984 | tf_op jit(solution)/shard_map/ppermute | solution.py:261
  77.1 9.7 %collective-permute-done.2 = f32[104,512]{1,0:T(8,128)S(1)} collective-permute-done((f32[104,512]{1,0:T(8,128)S(1)}, f32[104,512]{1,0:T(8,128)S(1)}, u32[]{:S(2)}, u32[]{:S(2)}) %collective-permute-start.2) | collective-permute-done | bytes 213024 | tf_op jit(solution)/shard_map/ppermute | solution.py:261
  87.0 11.6 %all_to_all.32 = f32[4,4,16,512]{3,2,1,0:T(8,128)S(1)} all-to-all(f32[4,4,16,512]{3,2,1,0:T(8,128)S(1)} %broadcast_in_dim.11), channel_id=1, replica_groups=mesh['y'=4,'zh'=4,'core'=2,'zl'=4,'x'=4] {'y'}, dimensions={0} | all-to-all | bytes 1048576 | tf_op jit(solution)/shard_map/all_to_all | solution.py:251
  98.7 18.4 %second_sums.1 = (f32[16,16384]{1,0:T(8,128)S(1)}, f32[4,72,512]{2,1,0:T(8,128)}) custom-call(f32[24,8192]{1,0:T(8,128)S(1)} %get-tuple-element.31.values_ref.codes_ref.mine_ref.my_codes_ref, f32[24,8192]{1,0:T(8,128)S(1)} %get-tuple-element.31.values_ref.codes_ref.mine_ref.my_codes_ref, ...), custom_call_target="tpu_custom_call" | custom-call | flops 17179869184 | bytes 2097152 | tf_op jit(solution)/shard_map/second_sums/pallas_call | solution.py:211
  117.1 3.5 %all-to-all-start.4 = ((f32[4,72,512]{2,1,0:T(8,128)}), f32[4,72,512]{2,1,0:T(8,128)S(1)}, u32[]{:S(2)}, u32[]{:S(2)}) async-start(f32[4,72,512]{2,1,0:T(8,128)} %get-tuple-element.11), calls=%async_computation.4 | async-start | bytes 1179648 | tf_op jit(solution)/shard_map/all_to_all | solution.py:265
  120.6 8.7 %all-to-all-done.4 = f32[4,72,512]{2,1,0:T(8,128)S(1)} async-done(((f32[4,72,512]{2,1,0:T(8,128)}), f32[4,72,512]{2,1,0:T(8,128)S(1)}, u32[]{:S(2)}, u32[]{:S(2)}) %all-to-all-start.4) | async-done | bytes 589856 | tf_op jit(solution)/shard_map/all_to_all | solution.py:265
  129.3 1.9 %collective-permute-start.3 = (f32[88,512]{1,0:T(8,128)S(1)}, f32[88,512]{1,0:T(8,128)S(1)}, u32[]{:S(2)}, u32[]{:S(2)}) collective-permute-start(f32[88,512]{1,0:T(8,128)S(1)} %pad_maximum_fusion.5), channel_id=1, source_target_pairs={{0,96},{16,48},{32,64},{48,16},{64,32},{80,112},{96,0},{112,80},{1... | collective-permute-start | bytes 540680 | tf_op jit(solution)/shard_map/ppermute | solution.py:261
  131.3 6.4 %collective-permute-start.4 = (f32[16,256]{1,0:T(8,128)S(1)}, f32[16,256]{1,0:T(8,128)S(1)}, u32[]{:S(2)}, u32[]{:S(2)}) collective-permute-start(f32[16,256]{1,0:T(8,128)S(1)} %get-tuple-element.40), channel_id=1, source_target_pairs={{0,16},{16,0},{1,17},{17,1},{2,18},{18,2},{3,19},{19,3},{4,20},{20... | collective-permute-start | bytes 49160 | tf_op jit(solution)/shard_map/ppermute | solution.py:255
  140.2 5.0 %collective-permute-start.5 = (f32[104,512]{1,0:T(8,128)S(1)}, f32[104,512]{1,0:T(8,128)S(1)}, u32[]{:S(2)}, u32[]{:S(2)}) collective-permute-start(f32[104,512]{1,0:T(8,128)S(1)} %pad_maximum_fusion.3), channel_id=1, source_target_pairs={{0,32},{16,112},{32,0},{48,80},{64,96},{80,48},{96,64},{112,16},{1... | collective-permute-start | bytes 638984 | tf_op jit(solution)/shard_map/ppermute | solution.py:261
  145.2 7.9 %collective-permute-done.5 = f32[104,512]{1,0:T(8,128)S(1)} collective-permute-done((f32[104,512]{1,0:T(8,128)S(1)}, f32[104,512]{1,0:T(8,128)S(1)}, u32[]{:S(2)}, u32[]{:S(2)}) %collective-permute-start.5) | collective-permute-done | bytes 213024 | tf_op jit(solution)/shard_map/ppermute | solution.py:261
  153.3 9.3 %all_to_all.33 = f32[4,4,16,512]{3,2,1,0:T(8,128)S(1)} all-to-all(f32[4,4,16,512]{3,2,1,0:T(8,128)S(1)} %broadcast_in_dim.12), channel_id=1, replica_groups=mesh['y'=4,'zh'=4,'core'=2,'zl'=4,'x'=4] {'y'}, dimensions={0} | all-to-all | bytes 1048576 | tf_op jit(solution)/shard_map/all_to_all | solution.py:251
  162.7 4.9 %last_lookup.2 = f32[24,8192]{1,0:T(8,128)S(1)} custom-call(f32[16,16384]{1,0:T(8,128)S(1)} %get-tuple-element.17.middle_ref, f32[24,8192]{1,0:T(8,128)S(1)} %collective-permute-done.values_ref.codes_ref.theirs_ref.their_codes_ref, f32[256,512]{1,0:T(8,128)S(1)} %bitcast.39, f32[8,8192]{1,0:T(8,128)S(1)} %broadcast_in_dim.14.refs_1_), custom_call_target="tpu_custom_call" | custom-call | flops 4294967296 | bytes 1048576 | tf_op jit(solution)/shard_map/last_lookup/pallas_call | solution.py:233
  167.6 11.7 %collective-permute-start.6 = (f32[24,8192]{1,0:T(8,128)S(1)}, f32[24,8192]{1,0:T(8,128)S(1)}, u32[]{:S(2)}, u32[]{:S(2)}) collective-permute-start(f32[24,8192]{1,0:T(8,128)S(1)} %last_lookup.2), channel_id=1, source_target_pairs={{0,16},{16,0},{1,17},{17,1},{2,18},{18,2},{3,19},{19,3},{4,20},{20... | collective-permute-start | bytes 2359304 | tf_op jit(solution)/shard_map/ppermute | solution.py:255
  179.3 4.8 %last_lookup.3 = f32[16,8192]{1,0:T(8,128)S(1)} custom-call(f32[16,16384]{1,0:T(8,128)S(1)} %get-tuple-element.17.middle_ref, f32[24,8192]{1,0:T(8,128)S(1)} %get-tuple-element.31.values_ref.codes_ref.mine_ref.my_codes_ref, f32[256,512]{1,0:T(8,128)S(1)} %bitcast.40), custom_call_target="tpu_custom_call" | custom-call | flops 4294967296 | bytes 1048576 | tf_op jit(solution)/shard_map/last_lookup/pallas_call | solution.py:233
  (75 shorter events, 7.7 us)
Async XLA Ops:
  0.6 1.0 copy-start
  11.5 6.5 %copy-start.2 = (s32[8192]{0:T(1024)S(1)}, s32[8192]{0:T(1024)}, u32[]{:S(2)}) copy-start(s32[8192]{0:T(1024)} %param.7) | copy-start | bytes 98308
  11.5 6.5 %copy-start.3 = (s32[8192]{0:T(1024)S(1)}, s32[8192]{0:T(1024)}, u32[]{:S(2)}) copy-start(s32[8192]{0:T(1024)} %param.6) | copy-start | bytes 98308
  11.5 6.6 %copy-start.4 = (f32[32,256]{1,0:T(8,128)S(1)}, f32[32,256]{1,0:T(8,128)}, u32[]{:S(2)}) copy-start(f32[32,256]{1,0:T(8,128)} %param.9) | copy-start | bytes 98308
  11.5 6.6 %copy-start.5 = (f32[32,256]{1,0:T(8,128)S(1)}, f32[32,256]{1,0:T(8,128)}, u32[]{:S(2)}) copy-start(f32[32,256]{1,0:T(8,128)} %param.8) | copy-start | bytes 98308
  12.3 10.7 %copy-start.1 = (bf16[32,8192]{1,0:T(8,128)(2,1)S(1)}, bf16[32,8192]{1,0:T(8,128)(2,1)}, u32[]{:S(2)}) copy-start(bf16[32,8192]{1,0:T(8,128)(2,1)} %e_ref.1) | copy-start | bytes 1572868
  12.3 10.5 %all-to-all-start.1 = ((f32[4,1,8192]{2,1,0:T(1,128)}), f32[4,1,8192]{2,1,0:T(1,128)S(1)}, u32[]{:S(2)}, u32[]{:S(2)}) async-start(f32[4,1,8192]{2,1,0:T(1,128)} %broadcast_in_dim.10), calls=%async_computation.1 | async-start | bytes 262144 | tf_op jit(solution)/shard_map/all_to_all | solution.py:251
  23.3 10.7 %collective-permute-start = (f32[24,8192]{1,0:T(8,128)S(1)}, f32[24,8192]{1,0:T(8,128)S(1)}, u32[]{:S(2)}, u32[]{:S(2)}) collective-permute-start(f32[24,8192]{1,0:T(8,128)S(1)} %get-tuple-element.32), channel_id=1, source_target_pairs={{0,16},{16,0},{1,17},{17,1},{2,18},{18,2},{3,19},{19,3},{4,20},{20... | collective-permute-start | bytes 2359304 | tf_op jit(solution)/shard_map/ppermute | solution.py:255
  39.1 13.8 %all-to-all-start.2 = ((f32[4,72,512]{2,1,0:T(8,128)}), f32[4,72,512]{2,1,0:T(8,128)S(1)}, u32[]{:S(2)}, u32[]{:S(2)}) async-start(f32[4,72,512]{2,1,0:T(8,128)} %first_sums.3), calls=%async_computation.2 | async-start | bytes 1179648 | tf_op jit(solution)/shard_map/all_to_all | solution.py:265
  52.9 17.4 %collective-permute-start.1 = (f32[88,512]{1,0:T(8,128)S(1)}, f32[88,512]{1,0:T(8,128)S(1)}, u32[]{:S(2)}, u32[]{:S(2)}) collective-permute-start(f32[88,512]{1,0:T(8,128)S(1)} %pad_maximum_fusion.4), channel_id=1, source_target_pairs={{0,32},{16,112},{32,0},{48,80},{64,96},{80,48},{96,64},{112,16},{1... | collective-permute-start | bytes 540680 | tf_op jit(solution)/shard_map/ppermute | solution.py:261
  70.4 16.4 %collective-permute-start.2 = (f32[104,512]{1,0:T(8,128)S(1)}, f32[104,512]{1,0:T(8,128)S(1)}, u32[]{:S(2)}, u32[]{:S(2)}) collective-permute-start(f32[104,512]{1,0:T(8,128)S(1)} %pad_maximum_fusion.2), channel_id=1, source_target_pairs={{0,96},{16,48},{32,64},{48,16},{64,32},{80,112},{96,0},{112,80},{1... | collective-permute-start | bytes 638984 | tf_op jit(solution)/shard_map/ppermute | solution.py:261
  117.1 12.2 %all-to-all-start.4 = ((f32[4,72,512]{2,1,0:T(8,128)}), f32[4,72,512]{2,1,0:T(8,128)S(1)}, u32[]{:S(2)}, u32[]{:S(2)}) async-start(f32[4,72,512]{2,1,0:T(8,128)} %get-tuple-element.11), calls=%async_computation.4 | async-start | bytes 1179648 | tf_op jit(solution)/shard_map/all_to_all | solution.py:265
  129.3 10.8 %collective-permute-start.3 = (f32[88,512]{1,0:T(8,128)S(1)}, f32[88,512]{1,0:T(8,128)S(1)}, u32[]{:S(2)}, u32[]{:S(2)}) collective-permute-start(f32[88,512]{1,0:T(8,128)S(1)} %pad_maximum_fusion.5), channel_id=1, source_target_pairs={{0,96},{16,48},{32,64},{48,16},{64,32},{80,112},{96,0},{112,80},{1... | collective-permute-start | bytes 540680 | tf_op jit(solution)/shard_map/ppermute | solution.py:261
  131.3 7.2 %collective-permute-start.4 = (f32[16,256]{1,0:T(8,128)S(1)}, f32[16,256]{1,0:T(8,128)S(1)}, u32[]{:S(2)}, u32[]{:S(2)}) collective-permute-start(f32[16,256]{1,0:T(8,128)S(1)} %get-tuple-element.40), channel_id=1, source_target_pairs={{0,16},{16,0},{1,17},{17,1},{2,18},{18,2},{3,19},{19,3},{4,20},{20... | collective-permute-start | bytes 49160 | tf_op jit(solution)/shard_map/ppermute | solution.py:255
  140.2 12.9 %collective-permute-start.5 = (f32[104,512]{1,0:T(8,128)S(1)}, f32[104,512]{1,0:T(8,128)S(1)}, u32[]{:S(2)}, u32[]{:S(2)}) collective-permute-start(f32[104,512]{1,0:T(8,128)S(1)} %pad_maximum_fusion.3), channel_id=1, source_target_pairs={{0,32},{16,112},{32,0},{48,80},{64,96},{80,48},{96,64},{112,16},{1... | collective-permute-start | bytes 638984 | tf_op jit(solution)/shard_map/ppermute | solution.py:261
  167.6 16.5 %collective-permute-start.6 = (f32[24,8192]{1,0:T(8,128)S(1)}, f32[24,8192]{1,0:T(8,128)S(1)}, u32[]{:S(2)}, u32[]{:S(2)}) collective-permute-start(f32[24,8192]{1,0:T(8,128)S(1)} %last_lookup.2), channel_id=1, source_target_pairs={{0,16},{16,0},{1,17},{17,1},{2,18},{18,2},{3,19},{19,3},{4,20},{20... | collective-permute-start | bytes 2359304 | tf_op jit(solution)/shard_map/ppermute | solution.py:255
